TPU v7x, 768 devices: a whole 4x8x12 slice. The times are simulated.
768 devices in a mesh: row: 32 (over z_hi, y), col: 6 (over z_lo, core), depth: 4 (over x).
Axes of the slice: x: 4, y: 8, z: 12 (z_hi: 4, z_lo: 3; z = z_hi * 3 + z_lo), core: 2. Of those that a mesh axis runs over, the one named last changes fastest.
Arguments:
- amplitudes: bfloat16 [192, 1536, 2048], P('row', 'col', 'depth'), may hold values from -6 to 6
- integrals: bfloat16 [2048, 2048], replicated, may hold values from -0.375 to 0.375
- pair_irreps: int32 [2048], replicated, may hold values from 0 to 7
- occ_fock: bfloat16 [192, 192], replicated, may hold values from -0.4375 to 0.4375
Outputs:
- residual: bfloat16 [192, 1536, 2048], P('row', 'col', 'depth')
All inputs are finite; a program needn't handle non-finite values.
Results may differ from a plain program's by a relative error of at most 0.0039.
Values may be sent and summed in bfloat16 or wider, within the bound.
No kernel may reach another device: no remote copies, remote signals or barrier semaphores. Data moves between devices by JAX's collectives and lax.ppermute only.
A program may use at most 64 MiB of HBM per device.

v0:
```python
import jax
import jax.numpy as jnp
from jax import lax
from jax.sharding import PartitionSpec as P


def masked_block(integrals, pair_irreps, row_start, row_count, col_count):
    block = lax.dynamic_slice(integrals, (row_start, 0), (row_count, col_count))
    labels_rows = lax.dynamic_slice_in_dim(pair_irreps, row_start, row_count, 0)
    same = labels_rows[:, None] == pair_irreps[None, :]
    return jnp.where(same, block, jnp.zeros_like(block))


def on_device(amplitudes, integrals, pair_irreps, occ_fock):
    local_i, local_j, share = amplitudes.shape
    whole_pairs = integrals.shape[0]
    depth_index = lax.axis_index("depth")
    offset = depth_index * share
    product = jnp.einsum(
        "ik,kmn->imn",
        occ_fock,
        lax.all_to_all(amplitudes, "row", split_axis=1, concat_axis=0, tiled=True),
        preferred_element_type=jnp.float32,
    )
    dressed_part = (-product).astype(jnp.bfloat16)
    dressed = lax.all_to_all(dressed_part, "row", split_axis=0, concat_axis=1, tiled=True)
    own_rows = masked_block(integrals, pair_irreps, offset, share, whole_pairs)
    partial_sum = jnp.dot(
        amplitudes.reshape(local_i * local_j, share), own_rows, preferred_element_type=jnp.float32
    )
    partial_sum = partial_sum.reshape(local_i, local_j, whole_pairs)
    ladder = lax.psum_scatter(partial_sum, "depth", scatter_dimension=2, tiled=True)
    return (ladder + dressed.astype(jnp.float32)).astype(jnp.bfloat16)


def solution(mesh):
    placed = (P("row", "col", "depth"), P(), P(), P())
    return jax.shard_map(
        on_device, mesh=mesh, in_specs=placed, out_specs=P("row", "col", "depth"), check_vma=False
    )
```

profile of v0, /device:TPU:136, one launch (start us, length us, event | category | flops | bytes accessed | tf_op | source)
XLA Modules:
  0.0 200.0 jit_solution(16071214383991574057)
XLA Ops:
  6.5 0.0 copy-start
  6.5 0.0 reduce-scatter.2.cloned.1.call-start
  6.5 0.8 dynamic_slice.6
  7.3 10.1 %fusion.1 = f32[2048,1536]{0,1:T(8,128)} fusion(bf16[1536,512]{1,0:T(8,128)(2,1)} %bitcast.24, bf16[2048,2048]{1,0:T(8,128)(2,1)} %param.5, s32[]{:T(128)S(6)} %select_n.8, s32[2048]{0:T(1024)} %param.6, s32[512]{0:T(512)S(1)} %dynamic_slice.6), kind=kOutput, calls=%fused_computation.5 | convolution fusion | flops 3223322624 | bytes 16263172 | tf_op jit(solution)/shard_map/dot_general | solution.py:28
  17.5 0.0 copy-start.1
  17.5 0.0 reduce-scatter.2.cloned.1.call-update
  17.5 1.4 copy-done.1
  18.9 0.9 copy.13
  19.8 96.0 %all_to_all.27 = bf16[6,256,512]{2,0,1:T(8,128)(2,1)S(1)} all-to-all(bf16[6,256,512]{2,0,1:T(8,128)(2,1)S(1)} %copy.13), channel_id=1, replica_groups=mesh['row'=32,'col'=6,'depth'=4] {'row'}, dimensions={1} | all-to-all | bytes 3145728 | tf_op jit(solution)/shard_map/all_to_all | solution.py:22
  115.7 0.7 copy.15
  116.4 0.0 copy-done
  116.4 1.3 negate_convert_fusion
  117.7 0.9 copy.17
  118.6 71.1 %all_to_all.28 = bf16[192,8,512]{2,1,0:T(8,128)(2,1)S(1)} all-to-all(bf16[192,8,512]{2,1,0:T(8,128)(2,1)S(1)} %copy.17), channel_id=1, replica_groups=mesh['row'=32,'col'=6,'depth'=4] {'row'}, dimensions={0} | all-to-all | bytes 3145728 | tf_op jit(solution)/shard_map/all_to_all | solution.py:26
  189.6 0.0 reduce-scatter.2.cloned.1.call-done
  189.6 3.6 %fusion = bf16[6,256,512]{2,1,0:T(8,128)(2,1)} fusion(f32[6,256,512]{2,1,0:T(8,128)} %reduce-scatter.2.cloned.1.call-done, bf16[32,6,8,512]{3,2,1,0:T(8,128)(2,1)S(1)} %bitcast.23), kind=kLoop, calls=%fused_computation.3 | loop fusion | flops 2359296 | bytes 6291456 | tf_op jit(solution)/shard_map/convert_element_type | solution.py:33
Async XLA Ops:
  6.5 109.9 %copy-start = (bf16[192,192]{1,0:T(8,128)(2,1)S(1)}, bf16[192,192]{1,0:T(8,128)(2,1)}, u32[]{:S(2)}) copy-start(bf16[192,192]{1,0:T(8,128)(2,1)} %param.7) | copy-start | bytes 221188
  6.5 183.1 %reduce-scatter.2.cloned.1.call-start = ((), (), s32[]{:S(2)}) async-start(), calls=%async_computation.3 | async-start | bytes 15728640 | tf_op jit(solution)/shard_map/reduce_scatter | solution.py:32
  17.5 1.4 copy-start.1
Sparse Core Ops, SparseCore 0:
  17.6 127.7 reduce-scatter.1
where the time goes:
time: 200 us
  blocking collectives  167 us (84%)
  between operations  13.4 us (7%)
  matrix products  11.4 us (6%)
  local copies, waits for them, and re-layouts  4.62 us (2%)
  other arithmetic  3.57 us (2%)
    all_to_all x1, blocking collectives, on_device(): lax.all_to_all(amplitudes, 'row', split_axis=1, concat_axis=0, tiled=True)  96 us
    all_to_all x1, blocking collectives, on_device(): lax.all_to_all(dressed_part, 'row', split_axis=0, concat_axis=1, tiled=True)  71.1 us
    dot_general x1, matrix products, on_device(): jnp.dot(amplitudes.reshape(local_i * local_j, share), own_rows, preferred...  10.1 us
  transfers between devices with their start and end apart: 1, of which 0 were waited for; matrix products, arithmetic and copies ran while one was open for 2% of the time, Pallas kernels for 0%

commit v1 on v0

v1 whole, which is shorter than its diff:
```python
import jax
import jax.numpy as jnp
from jax import lax
from jax.experimental import pallas as pl
from jax.experimental.pallas import tpu as pltpu
from jax.sharding import PartitionSpec as P


def ladder_kernel(parts_ref, masked_ref, out_ref):
    depth = parts_ref.shape[0]
    total = jnp.dot(parts_ref[0], masked_ref[0], preferred_element_type=jnp.float32)
    for d in range(1, depth):
        total += jnp.dot(parts_ref[d], masked_ref[d], preferred_element_type=jnp.float32)
    out_ref[...] = total


def ladder_product(parts, masked):
    depth, rows, share = parts.shape
    columns = masked.shape[2]
    steps = 6
    block = rows // steps
    return pl.pallas_call(
        ladder_kernel,
        grid=(steps,),
        in_specs=[
            pl.BlockSpec((depth, block, share), lambda r: (0, r, 0)),
            pl.BlockSpec((depth, share, columns), lambda r: (0, 0, 0)),
        ],
        out_specs=pl.BlockSpec((block, columns), lambda r: (r, 0)),
        out_shape=jax.ShapeDtypeStruct((rows, columns), jnp.float32),
        compiler_params=pltpu.CompilerParams(vmem_limit_bytes=24 * 1024 * 1024),
        cost_estimate=pl.CostEstimate(
            flops=2 * depth * rows * share * columns,
            bytes_accessed=2 * depth * share * (rows + columns) + 4 * rows * columns,
            transcendentals=0,
        ),
        name="ladder",
    )(parts, masked)


def on_device(amplitudes, integrals, pair_irreps, occ_fock):
    local_i, local_j, share = amplitudes.shape
    whole_pairs = integrals.shape[0]
    whole_i = occ_fock.shape[0]
    rows = whole_i // local_i
    depth = whole_pairs // share
    hub_j = local_j // rows
    offset = lax.axis_index("depth") * share

    gathered = lax.all_gather(amplitudes, "depth", axis=0, tiled=False)

    blocks = amplitudes.reshape(local_i, rows, hub_j, share).transpose(1, 0, 2, 3)
    arrived = lax.all_to_all(blocks, "row", split_axis=0, concat_axis=0)
    product = jnp.einsum(
        "ik,kmn->imn",
        occ_fock,
        arrived.reshape(whole_i, hub_j, share),
        preferred_element_type=jnp.float32,
    )
    dressed_part = (-product).astype(jnp.bfloat16).reshape(rows, local_i, hub_j, share)
    dressed = lax.all_to_all(dressed_part, "row", split_axis=0, concat_axis=0)
    dressed = dressed.transpose(1, 0, 2, 3).reshape(local_i, local_j, share)

    own_columns = lax.dynamic_slice(integrals, (0, offset), (whole_pairs, share))
    own_labels = lax.dynamic_slice_in_dim(pair_irreps, offset, share, 0)
    same = pair_irreps[:, None] == own_labels[None, :]
    masked = jnp.where(same, own_columns, jnp.zeros_like(own_columns))
    ladder = ladder_product(
        gathered.reshape(depth, local_i * local_j, share), masked.reshape(depth, share, share)
    ).reshape(local_i, local_j, share)
    return (ladder + dressed.astype(jnp.float32)).astype(jnp.bfloat16)


def solution(mesh):
    placed = (P("row", "col", "depth"), P(), P(), P())
    return jax.shard_map(
        on_device, mesh=mesh, in_specs=placed, out_specs=P("row", "col", "depth"), check_vma=False
    )
```

time: 200 us -> 169 us (0.84)
  the two profiles are of different devices: /device:TPU:136 before, /device:TPU:138 now
where the time goes in v1:
time: 169 us; the launch traced here: 168 us
  blocking collectives  79.4 us (47%)
  waiting for transfers between devices  51.1 us (30%)
  between operations  13.4 us (8%)
  local copies, waits for them, and re-layouts  7.36 us (4%)
  other arithmetic  5.97 us (4%)
  starting transfers between devices  5.12 us (3%)
  Pallas kernels  4.67 us (3%)
    all_to_all x1, blocking collectives, on_device(): arrived = lax.all_to_all(blocks, 'row', split_axis=0, concat_axis=0)  79.4 us
    all_to_all x1, waiting for transfers between devices, on_device(): dressed = lax.all_to_all(dressed_part, 'row', split_axis=0, concat_axis=0)  50.4 us
    all_to_all x1, starting transfers between devices, on_device(): dressed = lax.all_to_all(dressed_part, 'row', split_axis=0, concat_axis=0)  5.12 us
    unnamed x10, local copies, waits for them, and re-layouts  5.1 us
    pallas_call x1, Pallas kernels, ladder_product(): pl.pallas_call(ladder_kernel, grid=(steps,), in_specs=[pl.BlockSpec((dept...  4.67 us
  transfers between devices with their start and end apart: 2, of which 1 were waited for; matrix products, arithmetic and copies ran while one was open for 4% of the time, Pallas kernels for 3%

profile of v1, /device:TPU:138, one launch (start us, length us, event | category | flops | bytes accessed | tf_op | source)
XLA Modules:
  0.0 168.4 jit_solution(7915219133554656558)
XLA Ops:
  6.5 0.0 copy-start
  6.5 0.0 copy-start.3
  6.5 0.0 all-gather.3.cloned.1.call-start
  6.5 0.7 all-gather.3.cloned.1.call-update
  7.3 0.7 copy-done.3
  8.0 0.2 copy.13
  8.2 79.4 %all_to_all.10 = bf16[32,6,8,512]{3,2,1,0:T(8,128)(2,1)S(1)} all-to-all(bf16[32,6,8,512]{3,2,1,0:T(8,128)(2,1)S(1)} %copy.13), channel_id=1, replica_groups=mesh['row'=32,'col'=6,'depth'=4] {'row'}, dimensions={0} | all-to-all | bytes 3145728 | tf_op jit(solution)/shard_map/all_to_all | solution.py:53
  87.6 0.0 copy-done
  87.6 1.3 negate_convert_fusion
  88.9 2.0 %copy.15 = bf16[192,8,512]{2,1,0:T(8,128)(2,1)} copy(bf16[192,8,512]{2,0,1:T(8,128)(2,1)S(1)} %negate_convert_fusion) | data formatting | bytes 3145728 | tf_op jit(solution)/shard_map/convert_element_type | solution.py:60
  90.9 0.0 copy-start.4
  90.9 5.1 %all-to-all-start.1 = ((bf16[32,6,8,512]{3,2,1,0:T(8,128)(2,1)}), bf16[32,6,8,512]{3,2,1,0:T(8,128)(2,1)}, u32[]{:S(2)}, u32[]{:S(2)}) async-start(bf16[32,6,8,512]{3,2,1,0:T(8,128)(2,1)} %bitcast.7), calls=%async_computation.1 | async-start | bytes 3145728 | tf_op jit(solution)/shard_map/all_to_all | solution.py:61
  96.0 0.0 copy-done.4
  96.0 0.1 dynamic_slice.6
  96.1 2.9 %compare_select_fusion = bf16[2048,512]{1,0:T(8,128)(2,1)} fusion(bf16[2048,2048]{1,0:T(8,128)(2,1)} %param.5, s32[]{:T(128)S(6)} %select_n.8, s32[512]{0:T(512)S(1)} %dynamic_slice.6, s32[2048]{0:T(1024)S(1)} %copy-done.4), kind=kLoop, calls=%fused_computation | loop fusion | flops 2097152 | bytes 4204548 | tf_op jit(solution)/shard_map/jit(_where)/select_n | solution.py:67
  99.0 0.0 all-gather.3.cloned.1.call-done
  99.0 0.0 copy-start.1
  99.0 1.6 copy-done.1
  100.6 0.0 copy-start.2
  100.6 2.8 %copy-done.2 = bf16[24,256,512]{2,1,0:T(8,128)(2,1)S(1)} copy-done((bf16[24,256,512]{2,1,0:T(8,128)(2,1)S(1)}, bf16[24,256,512]{2,1,0:T(8,128)(2,1)}, u32[]{:S(2)}) %copy-start.2) | copy-done | bytes 6291480
  103.3 4.7 %ladder.1 = f32[1536,512]{1,0:T(8,128)S(1)} custom-call(bf16[4,1536,512]{2,1,0:T(8,128)(2,1)S(1)} %bitcast.20, bf16[4,512,512]{2,1,0:T(8,128)(2,1)S(1)} %bitcast.19), custom_call_target="tpu_custom_call" | custom-call | flops 3221225472 | bytes 11534336 | tf_op jit(solution)/shard_map/ladder/pallas_call | solution.py:22
  108.0 50.4 %all-to-all-done.1 = bf16[32,6,8,512]{3,2,1,0:T(8,128)(2,1)} async-done(((bf16[32,6,8,512]{3,2,1,0:T(8,128)(2,1)}), bf16[32,6,8,512]{3,2,1,0:T(8,128)(2,1)}, u32[]{:S(2)}, u32[]{:S(2)}) %all-to-all-start.1) | async-done | bytes 1572896 | tf_op jit(solution)/shard_map/all_to_all | solution.py:61
  158.5 3.1 %fusion = bf16[6,256,512]{2,1,0:T(8,128)(2,1)} fusion(f32[6,256,512]{2,1,0:T(8,128)S(1)} %bitcast.18, bf16[32,6,8,512]{3,2,1,0:T(8,128)(2,1)} %all-to-all-done.1), kind=kLoop, calls=%fused_computation.2 | loop fusion | flops 2359296 | bytes 6291456 | tf_op jit(solution)/shard_map/convert_element_type | solution.py:71
Async XLA Ops:
  6.5 81.1 %copy-start = (bf16[192,192]{1,0:T(8,128)(2,1)S(1)}, bf16[192,192]{1,0:T(8,128)(2,1)}, u32[]{:S(2)}) copy-start(bf16[192,192]{1,0:T(8,128)(2,1)} %param.7) | copy-start | bytes 221188
  6.5 1.4 copy-start.3
  6.5 92.4 %all-gather.3.cloned.1.call-start = ((), (), s32[]{:S(2)}) async-start(), calls=%async_computation.2 | async-start | bytes 7864320 | tf_op jit(solution)/shard_map/all_gather | solution.py:50
  90.9 5.1 %copy-start.4 = (s32[2048]{0:T(1024)S(1)}, s32[2048]{0:T(1024)}, u32[]{:S(2)}) copy-start(s32[2048]{0:T(1024)} %param.6) | copy-start | bytes 24580
  90.9 67.6 %all-to-all-start.1 = ((bf16[32,6,8,512]{3,2,1,0:T(8,128)(2,1)}), bf16[32,6,8,512]{3,2,1,0:T(8,128)(2,1)}, u32[]{:S(2)}, u32[]{:S(2)}) async-start(bf16[32,6,8,512]{3,2,1,0:T(8,128)(2,1)} %bitcast.7), calls=%async_computation.1 | async-start | bytes 3145728 | tf_op jit(solution)/shard_map/all_to_all | solution.py:61
  99.0 1.6 copy-start.1
  100.6 2.8 %copy-start.2 = (bf16[24,256,512]{2,1,0:T(8,128)(2,1)S(1)}, bf16[24,256,512]{2,1,0:T(8,128)(2,1)}, u32[]{:S(2)}) copy-start(bf16[24,256,512]{2,1,0:T(8,128)(2,1)} %all-gather.3.cloned.1.call-done) | copy-start | bytes 18874372
Sparse Core Ops, SparseCore 0:
  9.8 78.5 all-gather.2

commit v2 on v1

--- a/solution.py
+++ b/solution.py
@@ -6,27 +6,30 @@
 from jax.sharding import PartitionSpec as P
 
 
-def ladder_kernel(parts_ref, masked_ref, out_ref):
-    depth = parts_ref.shape[0]
-    total = jnp.dot(parts_ref[0], masked_ref[0], preferred_element_type=jnp.float32)
-    for d in range(1, depth):
-        total += jnp.dot(parts_ref[d], masked_ref[d], preferred_element_type=jnp.float32)
+def ladder_kernel(order_ref, *refs):
+    part_refs, masked_ref, out_ref = refs[:-2], refs[-2], refs[-1]
+    total = None
+    for d, part_ref in enumerate(part_refs):
+        term = jnp.dot(part_ref[...], masked_ref[order_ref[d]], preferred_element_type=jnp.float32)
+        total = term if total is None else total + term
     out_ref[...] = total
 
 
-def ladder_product(parts, masked):
-    depth, rows, share = parts.shape
+def ladder_product(order, parts, masked):
+    depth = len(parts)
+    rows, share = parts[0].shape
     columns = masked.shape[2]
     steps = 6
     block = rows // steps
     return pl.pallas_call(
         ladder_kernel,
-        grid=(steps,),
-        in_specs=[
-            pl.BlockSpec((depth, block, share), lambda r: (0, r, 0)),
-            pl.BlockSpec((depth, share, columns), lambda r: (0, 0, 0)),
-        ],
-        out_specs=pl.BlockSpec((block, columns), lambda r: (r, 0)),
+        grid_spec=pltpu.PrefetchScalarGridSpec(
+            num_scalar_prefetch=1,
+            grid=(steps,),
+            in_specs=[pl.BlockSpec((block, share), lambda r, order: (r, 0))] * depth
+            + [pl.BlockSpec((depth, share, columns), lambda r, order: (0, 0, 0))],
+            out_specs=pl.BlockSpec((block, columns), lambda r, order: (r, 0)),
+        ),
         out_shape=jax.ShapeDtypeStruct((rows, columns), jnp.float32),
         compiler_params=pltpu.CompilerParams(vmem_limit_bytes=24 * 1024 * 1024),
         cost_estimate=pl.CostEstimate(
@@ -35,7 +38,7 @@
             transcendentals=0,
         ),
         name="ladder",
-    )(parts, masked)
+    )(order, *parts, masked)
 
 
 def on_device(amplitudes, integrals, pair_irreps, occ_fock):
@@ -47,7 +50,11 @@
     hub_j = local_j // rows
     offset = lax.axis_index("depth") * share
 
-    gathered = lax.all_gather(amplitudes, "depth", axis=0, tiled=False)
+    parts = [amplitudes] + [
+        lax.ppermute(amplitudes, "depth", [(d, (d + step) % depth) for d in range(depth)])
+        for step in range(1, depth)
+    ]
+    order = (lax.axis_index("depth") - jnp.arange(depth, dtype=jnp.int32) + depth) % depth
 
     blocks = amplitudes.reshape(local_i, rows, hub_j, share).transpose(1, 0, 2, 3)
     arrived = lax.all_to_all(blocks, "row", split_axis=0, concat_axis=0)
@@ -66,7 +73,9 @@
     same = pair_irreps[:, None] == own_labels[None, :]
     masked = jnp.where(same, own_columns, jnp.zeros_like(own_columns))
     ladder = ladder_product(
-        gathered.reshape(depth, local_i * local_j, share), masked.reshape(depth, share, share)
+        order,
+        [part.reshape(local_i * local_j, share) for part in parts],
+        masked.reshape(depth, share, share),
     ).reshape(local_i, local_j, share)
     return (ladder + dressed.astype(jnp.float32)).astype(jnp.bfloat16)
 

time: 169 us -> 180 us (1.065)
  the two profiles are of different devices: /device:TPU:138 before, /device:TPU:67 now
where the time goes in v2:
time: 180 us; the launch traced here: 179 us
  blocking collectives  78.1 us (43%)
  waiting for transfers between devices  63.7 us (35%)
  starting transfers between devices  18.1 us (10%)
  Pallas kernels  6.56 us (4%)
  local copies, waits for them, and re-layouts  6.27 us (3%)
  other arithmetic  5.1 us (3%)
    all_to_all x1, blocking collectives, on_device(): arrived = lax.all_to_all(blocks, 'row', split_axis=0, concat_axis=0)  78.1 us
    ppermute x3, waiting for transfers between devices, on_device(): lax.ppermute(amplitudes, 'depth', [(d, (d + step) % depth) for d in range...  63.7 us
    ppermute x3, starting transfers between devices, on_device(): lax.ppermute(amplitudes, 'depth', [(d, (d + step) % depth) for d in range...  9.65 us
    all_to_all x1, starting transfers between devices, on_device(): dressed = lax.all_to_all(dressed_part, 'row', split_axis=0, concat_axis=0)  8.47 us
    pallas_call x1, Pallas kernels, ladder_product(): pl.pallas_call(ladder_kernel, grid_spec=pltpu.PrefetchScalarGridSpec(num_...  6.56 us
  transfers between devices with their start and end apart: 4, of which 3 were waited for; matrix products, arithmetic and copies ran while one was open for 1% of the time, Pallas kernels for 4%

profile of v2, /device:TPU:67, one launch (start us, length us, event | category | flops | bytes accessed | tf_op | source)
XLA Modules:
  0.0 179.2 jit_solution(6078688910971215937)
XLA Ops:
  0.0 0.0 copy-start
  0.0 1.6 copy.13
  1.6 78.1 %all_to_all.10 = bf16[32,6,8,512]{3,2,1,0:T(8,128)(2,1)S(1)} all-to-all(bf16[32,6,8,512]{3,2,1,0:T(8,128)(2,1)S(1)} %copy.13), channel_id=1, replica_groups=mesh['row'=32,'col'=6,'depth'=4] {'row'}, dimensions={0} | all-to-all | bytes 3145728 | tf_op jit(solution)/shard_map/all_to_all | solution.py:60
  79.7 0.0 copy-done
  79.7 1.3 negate_convert_fusion
  81.0 2.0 %copy.15 = bf16[192,8,512]{2,1,0:T(8,128)(2,1)} copy(bf16[192,8,512]{2,0,1:T(8,128)(2,1)S(1)} %negate_convert_fusion) | data formatting | bytes 3145728 | tf_op jit(solution)/shard_map/convert_element_type | solution.py:67
  83.0 0.0 copy-start.1
  83.0 8.5 %all-to-all-start.1 = ((bf16[32,6,8,512]{3,2,1,0:T(8,128)(2,1)}), bf16[32,6,8,512]{3,2,1,0:T(8,128)(2,1)}, u32[]{:S(2)}, u32[]{:S(2)}) async-start(bf16[32,6,8,512]{3,2,1,0:T(8,128)(2,1)} %bitcast.10), calls=%async_computation.1 | async-start | bytes 3145728 | tf_op jit(solution)/shard_map/all_to_all | solution.py:68
  91.5 0.0 copy-done.1
  91.5 3.1 %collective-permute-start = (bf16[6,256,512]{2,1,0:T(8,128)(2,1)S(1)}, bf16[6,256,512]{2,1,0:T(8,128)(2,1)S(1)}, u32[]{:S(2)}, u32[]{:S(2)}) collective-permute-start(bf16[6,256,512]{2,1,0:T(8,128)(2,1)S(1)} %copy-done.1), channel_id=1, source_target_pairs={{0,1},{1,2},{2,3},{3,0},{4,5},{5,6},{6,7},{7,4},{8,9},{9,10},{10,1... | collective-permute-start | bytes 4718600 | tf_op jit(solution)/shard_map/ppermute | solution.py:54
  94.6 2.7 %collective-permute-start.1 = (bf16[6,256,512]{2,1,0:T(8,128)(2,1)S(1)}, bf16[6,256,512]{2,1,0:T(8,128)(2,1)}, u32[]{:S(2)}, u32[]{:S(2)}) collective-permute-start(bf16[6,256,512]{2,1,0:T(8,128)(2,1)S(1)} %copy-done.1), channel_id=1, source_target_pairs={{0,2},{1,3},{2,0},{3,1},{4,6},{5,7},{6,4},{7,5},{8,10},{9,11},{10,... | collective-permute-start | bytes 4718600 | tf_op jit(solution)/shard_map/ppermute | solution.py:54
  97.4 3.8 %collective-permute-start.2 = (bf16[6,256,512]{2,1,0:T(8,128)(2,1)S(1)}, bf16[6,256,512]{2,1,0:T(8,128)(2,1)}, u32[]{:S(2)}, u32[]{:S(2)}) collective-permute-start(bf16[6,256,512]{2,1,0:T(8,128)(2,1)S(1)} %copy-done.1), channel_id=1, source_target_pairs={{0,3},{1,0},{2,1},{3,2},{4,7},{5,4},{6,5},{7,6},{8,11},{9,8},{10,9... | collective-permute-start | bytes 4718600 | tf_op jit(solution)/shard_map/ppermute | solution.py:54
  101.2 0.0 copy-done.5
  101.2 0.1 dynamic_slice.6
  101.3 2.0 %compare_select_fusion = bf16[2048,512]{1,0:T(8,128)(2,1)S(1)} fusion(bf16[2048,2048]{1,0:T(8,128)(2,1)} %param.5, s32[]{:T(128)S(6)} %select_n.16, s32[512]{0:T(512)S(1)} %dynamic_slice.6, s32[2048]{0:T(1024)S(1)} %copy-done.5), kind=kLoop, calls=%fused_computation | loop fusion | flops 2097152 | bytes 4204548 | tf_op jit(solution)/shard_map/jit(_where)/select_n | solution.py:74
  103.3 24.8 %collective-permute-done = bf16[6,256,512]{2,1,0:T(8,128)(2,1)S(1)} collective-permute-done((bf16[6,256,512]{2,1,0:T(8,128)(2,1)S(1)}, bf16[6,256,512]{2,1,0:T(8,128)(2,1)S(1)}, u32[]{:S(2)}, u32[]{:S(2)}) %collective-permute-start) | collective-permute-done | bytes 1572896 | tf_op jit(solution)/shard_map/ppermute | solution.py:54
  128.1 1.1 copy-done.3
  129.2 3.3 %collective-permute-done.1 = bf16[6,256,512]{2,1,0:T(8,128)(2,1)} collective-permute-done((bf16[6,256,512]{2,1,0:T(8,128)(2,1)S(1)}, bf16[6,256,512]{2,1,0:T(8,128)(2,1)}, u32[]{:S(2)}, u32[]{:S(2)}) %collective-permute-start.1) | collective-permute-done | bytes 1572896 | tf_op jit(solution)/shard_map/ppermute | solution.py:54
  132.5 35.7 %collective-permute-done.2 = bf16[6,256,512]{2,1,0:T(8,128)(2,1)} collective-permute-done((bf16[6,256,512]{2,1,0:T(8,128)(2,1)S(1)}, bf16[6,256,512]{2,1,0:T(8,128)(2,1)}, u32[]{:S(2)}, u32[]{:S(2)}) %collective-permute-start.2) | collective-permute-done | bytes 1572896 | tf_op jit(solution)/shard_map/ppermute | solution.py:54
  168.2 0.0 copy-done.2
  168.2 1.4 copy-done.4
  169.6 6.6 %ladder.1 = f32[1536,512]{1,0:T(8,128)S(1)} custom-call(s32[4]{0:T(128)S(1)} %and_select_fusion.order_ref, bf16[1536,512]{1,0:T(8,128)(2,1)S(1)} %bitcast.24, bf16[1536,512]{1,0:T(8,128)(2,1)S(1)} %bitcast.25, bf16[1536,512]{1,0:T(8,128)(2,1)} %bitcast.2.refs_2_, bf16[1536,512]{1,0:T(8,128)(2,1)} %bitcast.3.refs_3_, bf16[4,512,512]{2,1,0:T(8,128)(2,1)S(1)} %bitcast.22), custom_call_target="tpu_custom_call" | custom-call | flops 3221225472 | bytes 11534336 | tf_op jit(solution)/shard_map/ladder/pallas_call | solution.py:24
  176.1 0.0 all-to-all-done.1
  176.2 3.1 %fusion = bf16[6,256,512]{2,1,0:T(8,128)(2,1)} fusion(f32[6,256,512]{2,1,0:T(8,128)S(1)} %bitcast.21, bf16[32,6,8,512]{3,2,1,0:T(8,128)(2,1)} %all-to-all-done.1), kind=kLoop, calls=%fused_computation.2 | loop fusion | flops 2359296 | bytes 6291456 | tf_op jit(solution)/shard_map/convert_element_type | solution.py:80
  (5 shorter events, 0.0 us)
Async XLA Ops:
  0.0 79.7 %copy-start = (bf16[192,192]{1,0:T(8,128)(2,1)S(1)}, bf16[192,192]{1,0:T(8,128)(2,1)}, u32[]{:S(2)}) copy-start(bf16[192,192]{1,0:T(8,128)(2,1)} %param.7) | copy-start | bytes 221188
  83.0 8.5 %copy-start.1 = (bf16[6,256,512]{2,1,0:T(8,128)(2,1)S(1)}, bf16[6,256,512]{2,1,0:T(8,128)(2,1)}, u32[]{:S(2)}) copy-start(bf16[6,256,512]{2,1,0:T(8,128)(2,1)} %param.4) | copy-start | bytes 4718596
  83.0 18.2 %copy-start.5 = (s32[2048]{0:T(1024)S(1)}, s32[2048]{0:T(1024)}, u32[]{:S(2)}) copy-start(s32[2048]{0:T(1024)} %param.6) | copy-start | bytes 24580
  83.0 93.1 %all-to-all-start.1 = ((bf16[32,6,8,512]{3,2,1,0:T(8,128)(2,1)}), bf16[32,6,8,512]{3,2,1,0:T(8,128)(2,1)}, u32[]{:S(2)}, u32[]{:S(2)}) async-start(bf16[32,6,8,512]{3,2,1,0:T(8,128)(2,1)} %bitcast.10), calls=%async_computation.1 | async-start | bytes 3145728 | tf_op jit(solution)/shard_map/all_to_all | solution.py:68
  91.5 36.6 %collective-permute-start = (bf16[6,256,512]{2,1,0:T(8,128)(2,1)S(1)}, bf16[6,256,512]{2,1,0:T(8,128)(2,1)S(1)}, u32[]{:S(2)}, u32[]{:S(2)}) collective-permute-start(bf16[6,256,512]{2,1,0:T(8,128)(2,1)S(1)} %copy-done.1), channel_id=1, source_target_pairs={{0,1},{1,2},{2,3},{3,0},{4,5},{5,6},{6,7},{7,4},{8,9},{9,10},{10,1... | collective-permute-start | bytes 4718600 | tf_op jit(solution)/shard_map/ppermute | solution.py:54
  94.6 37.9 %collective-permute-start.1 = (bf16[6,256,512]{2,1,0:T(8,128)(2,1)S(1)}, bf16[6,256,512]{2,1,0:T(8,128)(2,1)}, u32[]{:S(2)}, u32[]{:S(2)}) collective-permute-start(bf16[6,256,512]{2,1,0:T(8,128)(2,1)S(1)} %copy-done.1), channel_id=1, source_target_pairs={{0,2},{1,3},{2,0},{3,1},{4,6},{5,7},{6,4},{7,5},{8,10},{9,11},{10,... | collective-permute-start | bytes 4718600 | tf_op jit(solution)/shard_map/ppermute | solution.py:54
  97.4 70.8 %collective-permute-start.2 = (bf16[6,256,512]{2,1,0:T(8,128)(2,1)S(1)}, bf16[6,256,512]{2,1,0:T(8,128)(2,1)}, u32[]{:S(2)}, u32[]{:S(2)}) collective-permute-start(bf16[6,256,512]{2,1,0:T(8,128)(2,1)S(1)} %copy-done.1), channel_id=1, source_target_pairs={{0,3},{1,0},{2,1},{3,2},{4,7},{5,4},{6,5},{7,6},{8,11},{9,8},{10,9... | collective-permute-start | bytes 4718600 | tf_op jit(solution)/shard_map/ppermute | solution.py:54
  101.3 66.9 %copy-start.2 = (bf16[6,256,512]{2,1,0:T(8,128)(2,1)S(1)}, bf16[6,256,512]{2,1,0:T(8,128)(2,1)}, u32[]{:S(2)}) copy-start(bf16[6,256,512]{2,1,0:T(8,128)(2,1)} %param.4) | copy-start | bytes 4718596
  128.1 1.1 copy-start.3
  168.2 1.4 copy-start.4

commit v3 on v2

--- a/solution.py
+++ b/solution.py
@@ -6,28 +6,36 @@
 from jax.sharding import PartitionSpec as P
 
 
-def ladder_kernel(order_ref, *refs):
-    part_refs, masked_ref, out_ref = refs[:-2], refs[-2], refs[-1]
-    total = None
-    for d, part_ref in enumerate(part_refs):
-        term = jnp.dot(part_ref[...], masked_ref[order_ref[d]], preferred_element_type=jnp.float32)
-        total = term if total is None else total + term
+def ladder_kernel(order_ref, own_ref, below_ref, above_ref, far_low_ref, far_high_ref, masked_ref, out_ref):
+    low = pl.program_id(0) < pl.num_programs(0) // 2
+    far = jnp.where(low, far_low_ref[...], far_high_ref[...])
+    total = jnp.dot(own_ref[...], masked_ref[order_ref[0]], preferred_element_type=jnp.float32)
+    total += jnp.dot(below_ref[...], masked_ref[order_ref[1]], preferred_element_type=jnp.float32)
+    total += jnp.dot(above_ref[...], masked_ref[order_ref[3]], preferred_element_type=jnp.float32)
+    total += jnp.dot(far, masked_ref[order_ref[2]], preferred_element_type=jnp.float32)
     out_ref[...] = total
 
 
-def ladder_product(order, parts, masked):
-    depth = len(parts)
-    rows, share = parts[0].shape
-    columns = masked.shape[2]
+def ladder_product(order, own, below, above, far_low, far_high, masked):
+    depth, share, columns = masked.shape
+    rows = own.shape[0]
     steps = 6
+    half = steps // 2
     block = rows // steps
+    whole = pl.BlockSpec((block, share), lambda r, order: (r, 0))
     return pl.pallas_call(
         ladder_kernel,
         grid_spec=pltpu.PrefetchScalarGridSpec(
             num_scalar_prefetch=1,
             grid=(steps,),
-            in_specs=[pl.BlockSpec((block, share), lambda r, order: (r, 0))] * depth
-            + [pl.BlockSpec((depth, share, columns), lambda r, order: (0, 0, 0))],
+            in_specs=[
+                whole,
+                whole,
+                whole,
+                pl.BlockSpec((block, share), lambda r, order: (jnp.minimum(r, half - 1), 0)),
+                pl.BlockSpec((block, share), lambda r, order: (jnp.maximum(r - half, 0), 0)),
+                pl.BlockSpec((depth, share, columns), lambda r, order: (0, 0, 0)),
+            ],
             out_specs=pl.BlockSpec((block, columns), lambda r, order: (r, 0)),
         ),
         out_shape=jax.ShapeDtypeStruct((rows, columns), jnp.float32),
@@ -38,7 +46,11 @@
             transcendentals=0,
         ),
         name="ladder",
-    )(order, *parts, masked)
+    )(order, own, below, above, far_low, far_high, masked)
+
+
+def shift(block, depth, step):
+    return lax.ppermute(block, "depth", [(d, (d + step) % depth) for d in range(depth)])
 
 
 def on_device(amplitudes, integrals, pair_irreps, occ_fock):
@@ -50,14 +62,15 @@
     hub_j = local_j // rows
     offset = lax.axis_index("depth") * share
 
-    parts = [amplitudes] + [
-        lax.ppermute(amplitudes, "depth", [(d, (d + step) % depth) for d in range(depth)])
-        for step in range(1, depth)
-    ]
+    below = shift(amplitudes, depth, 1)
+    above = shift(amplitudes, depth, -1)
     order = (lax.axis_index("depth") - jnp.arange(depth, dtype=jnp.int32) + depth) % depth
 
     blocks = amplitudes.reshape(local_i, rows, hub_j, share).transpose(1, 0, 2, 3)
     arrived = lax.all_to_all(blocks, "row", split_axis=0, concat_axis=0)
+    arrived, below, above = lax.optimization_barrier((arrived, below, above))
+    far_low = shift(below[: local_i // 2], depth, 1)
+    far_high = shift(above[local_i // 2 :], depth, -1)
     product = jnp.einsum(
         "ik,kmn->imn",
         occ_fock,
@@ -74,7 +87,7 @@
     masked = jnp.where(same, own_columns, jnp.zeros_like(own_columns))
     ladder = ladder_product(
         order,
-        [part.reshape(local_i * local_j, share) for part in parts],
+        *(part.reshape(-1, share) for part in (amplitudes, below, above, far_low, far_high)),
         masked.reshape(depth, share, share),
     ).reshape(local_i, local_j, share)
     return (ladder + dressed.astype(jnp.float32)).astype(jnp.bfloat16)

time: 180 us -> 169 us (0.939)
  the two profiles are of different devices: /device:TPU:67 before, /device:TPU:141 now
where the time goes in v3:
time: 169 us; the launch traced here: 168 us
  waiting for transfers between devices  109 us (64%)
  starting transfers between devices  33.2 us (20%)
  local copies, waits for them, and re-layouts  12 us (7%)
  Pallas kernels  6.29 us (4%)
  other arithmetic  5.13 us (3%)
  matrix products  2.66 us (2%)
    ppermute x4, waiting for transfers between devices, shift(): lax.ppermute(block, 'depth', [(d, (d + step) % depth) for d in range(dept...  46 us
    all_to_all x1, waiting for transfers between devices, on_device(): dressed = lax.all_to_all(dressed_part, 'row', split_axis=0, concat_axis=0)  36.2 us
    all_to_all x1, waiting for transfers between devices, on_device(): arrived = lax.all_to_all(blocks, 'row', split_axis=0, concat_axis=0)  26.8 us
    all_to_all x1, starting transfers between devices, on_device(): arrived = lax.all_to_all(blocks, 'row', split_axis=0, concat_axis=0)  17.6 us
    ppermute x4, starting transfers between devices, shift(): lax.ppermute(block, 'depth', [(d, (d + step) % depth) for d in range(dept...  10.6 us
    pallas_call x1, Pallas kernels, ladder_product(): pl.pallas_call(ladder_kernel, grid_spec=pltpu.PrefetchScalarGridSpec(num_...  6.29 us
    all_to_all x1, starting transfers between devices, on_device(): dressed = lax.all_to_all(dressed_part, 'row', split_axis=0, concat_axis=0)  5.05 us
    unnamed x20, local copies, waits for them, and re-layouts  4.09 us
  transfers between devices with their start and end apart: 6, of which 6 were waited for; matrix products, arithmetic and copies ran while one was open for 3% of the time, Pallas kernels for 4%

profile of v3, /device:TPU:141, one launch (start us, length us, event | category | flops | bytes accessed | tf_op | source)
XLA Modules:
  0.0 168.4 jit_solution(14157720952983333079)
XLA Ops:
  0.0 2.8 %copy.13 = bf16[32,6,8,512]{3,2,1,0:T(8,128)(2,1)} copy(bf16[32,6,8,512]{3,2,0,1:T(8,128)(2,1)} %bitcast.26) | data formatting | bytes 3145728 | tf_op jit(solution)/shard_map/transpose | solution.py:69
  2.8 17.6 %all-to-all-start = ((bf16[32,6,8,512]{3,2,1,0:T(8,128)(2,1)}), bf16[32,6,8,512]{3,2,1,0:T(8,128)(2,1)}, u32[]{:S(2)}, u32[]{:S(2)}) async-start(bf16[32,6,8,512]{3,2,1,0:T(8,128)(2,1)} %copy.13), calls=%async_computation | async-start | bytes 3145728 | tf_op jit(solution)/shard_map/all_to_all | solution.py:70
  20.4 2.2 %collective-permute-start.1 = (bf16[6,256,512]{2,1,0:T(8,128)(2,1)S(1)}, bf16[6,256,512]{2,1,0:T(8,128)(2,1)S(1)}, u32[]{:S(2)}, u32[]{:S(2)}) collective-permute-start(bf16[6,256,512]{2,1,0:T(8,128)(2,1)S(1)} %copy-done.1), channel_id=1, source_target_pairs={{0,3},{1,0},{2,1},{3,2},{4,7},{5,4},{6,5},{7,6},{8,11},{9,8},{10,9... | collective-permute-start | bytes 4718600 | tf_op jit(solution)/shard_map/ppermute | solution.py:53
  22.6 3.1 %collective-permute-start = (bf16[6,256,512]{2,1,0:T(8,128)(2,1)S(1)}, bf16[6,256,512]{2,1,0:T(8,128)(2,1)}, u32[]{:S(2)}, u32[]{:S(2)}) collective-permute-start(bf16[6,256,512]{2,1,0:T(8,128)(2,1)S(1)} %copy-done.1), channel_id=1, source_target_pairs={{0,1},{1,2},{2,3},{3,0},{4,5},{5,6},{6,7},{7,4},{8,9},{9,10},{10,1... | collective-permute-start | bytes 4718600 | tf_op jit(solution)/shard_map/ppermute | solution.py:53
  25.7 31.3 %collective-permute-done.1 = bf16[6,256,512]{2,1,0:T(8,128)(2,1)S(1)} collective-permute-done((bf16[6,256,512]{2,1,0:T(8,128)(2,1)S(1)}, bf16[6,256,512]{2,1,0:T(8,128)(2,1)S(1)}, u32[]{:S(2)}, u32[]{:S(2)}) %collective-permute-start.1) | collective-permute-done | bytes 1572896 | tf_op jit(solution)/shard_map/ppermute | solution.py:53
  57.1 1.9 %collective-permute-done = bf16[6,256,512]{2,1,0:T(8,128)(2,1)} collective-permute-done((bf16[6,256,512]{2,1,0:T(8,128)(2,1)S(1)}, bf16[6,256,512]{2,1,0:T(8,128)(2,1)}, u32[]{:S(2)}, u32[]{:S(2)}) %collective-permute-start) | collective-permute-done | bytes 1572896 | tf_op jit(solution)/shard_map/ppermute | solution.py:53
  59.0 26.8 %all-to-all-done = bf16[32,6,8,512]{3,2,1,0:T(8,128)(2,1)} async-done(((bf16[32,6,8,512]{3,2,1,0:T(8,128)(2,1)}), bf16[32,6,8,512]{3,2,1,0:T(8,128)(2,1)}, u32[]{:S(2)}, u32[]{:S(2)}) %all-to-all-start) | async-done | bytes 1572896 | tf_op jit(solution)/shard_map/all_to_all | solution.py:70
  85.8 2.7 %fusion.2 = bf16[192,8,512]{2,0,1:T(8,128)(2,1)S(1)} fusion(bf16[192,8,512]{2,1,0:T(8,128)(2,1)} %bitcast.9, bf16[192,192]{1,0:T(8,128)(2,1)S(1)} %copy-done), kind=kOutput, calls=%fused_computation.6 | convolution fusion | flops 303562752 | bytes 3219456 | tf_op jit(solution)/shard_map/ik,kmn->imn/dot_general | solution.py:74
  88.4 2.0 %copy.15 = bf16[192,8,512]{2,1,0:T(8,128)(2,1)} copy(bf16[192,8,512]{2,0,1:T(8,128)(2,1)S(1)} %fusion.2) | data formatting | bytes 3145728 | tf_op jit(solution)/shard_map/convert_element_type | solution.py:80
  90.4 5.0 %all-to-all-start.1 = ((bf16[32,6,8,512]{3,2,1,0:T(8,128)(2,1)}), bf16[32,6,8,512]{3,2,1,0:T(8,128)(2,1)}, u32[]{:S(2)}, u32[]{:S(2)}) async-start(bf16[32,6,8,512]{3,2,1,0:T(8,128)(2,1)} %bitcast.12), calls=%async_computation.1 | async-start | bytes 3145728 | tf_op jit(solution)/shard_map/all_to_all | solution.py:81
  95.5 2.1 %slice.6 = bf16[3,256,512]{2,1,0:T(8,128)(2,1)} slice(bf16[6,256,512]{2,1,0:T(8,128)(2,1)} %collective-permute-done), slice={[0:3], [0:256], [0:512]} | slice | bytes 1572864 | tf_op jit(solution)/shard_map/slice | solution.py:72
  97.6 0.9 slice.7
  98.6 2.2 %collective-permute-start.3 = (bf16[3,256,512]{2,1,0:T(8,128)(2,1)}, bf16[3,256,512]{2,1,0:T(8,128)(2,1)S(1)}, u32[]{:S(2)}, u32[]{:S(2)}) collective-permute-start(bf16[3,256,512]{2,1,0:T(8,128)(2,1)} %slice.7), channel_id=1, source_target_pairs={{0,3},{1,0},{2,1},{3,2},{4,7},{5,4},{6,5},{7,6},{8,11},{9,8},{10,9... | collective-permute-start | bytes 2359304 | tf_op jit(solution)/shard_map/ppermute | solution.py:53
  100.7 3.1 %collective-permute-start.2 = (bf16[3,256,512]{2,1,0:T(8,128)(2,1)}, bf16[3,256,512]{2,1,0:T(8,128)(2,1)S(1)}, u32[]{:S(2)}, u32[]{:S(2)}) collective-permute-start(bf16[3,256,512]{2,1,0:T(8,128)(2,1)} %slice.6), channel_id=1, source_target_pairs={{0,1},{1,2},{2,3},{3,0},{4,5},{5,6},{6,7},{7,4},{8,9},{9,10},{10,1... | collective-permute-start | bytes 2359304 | tf_op jit(solution)/shard_map/ppermute | solution.py:53
  104.0 2.0 %compare_select_fusion = bf16[2048,512]{1,0:T(8,128)(2,1)S(1)} fusion(bf16[2048,2048]{1,0:T(8,128)(2,1)} %param.5, s32[]{:T(128)S(6)} %select_n.16, s32[512]{0:T(512)S(1)} %dynamic_slice.6, s32[2048]{0:T(1024)S(1)} %copy-done.9), kind=kLoop, calls=%fused_computation | loop fusion | flops 2097152 | bytes 4204548 | tf_op jit(solution)/shard_map/jit(_where)/select_n | solution.py:87
  106.0 11.8 %collective-permute-done.3 = bf16[3,256,512]{2,1,0:T(8,128)(2,1)S(1)} collective-permute-done((bf16[3,256,512]{2,1,0:T(8,128)(2,1)}, bf16[3,256,512]{2,1,0:T(8,128)(2,1)S(1)}, u32[]{:S(2)}, u32[]{:S(2)}) %collective-permute-start.3) | collective-permute-done | bytes 786464 | tf_op jit(solution)/shard_map/ppermute | solution.py:53
  117.8 0.9 copy-done.5
  118.7 1.0 collective-permute-done.2
  119.7 0.9 copy-done.7
  120.6 1.1 copy-done.6
  121.7 1.1 copy-done.8
  122.8 6.3 %ladder.1 = f32[1536,512]{1,0:T(8,128)S(1)} custom-call(s32[4]{0:T(128)S(1)} %and_select_fusion.order_ref, bf16[1536,512]{1,0:T(8,128)(2,1)S(1)} %bitcast.27, bf16[1536,512]{1,0:T(8,128)(2,1)} %bitcast.3.below_ref, bf16[1536,512]{1,0:T(8,128)(2,1)S(1)} %bitcast.28, bf16[768,512]{1,0:T(8,128)(2,1)S(1)} %bitcast.30, bf16[768,512]{1,0:T(8,128)(2,1)S(1)} %bitcast.29, ...), custom_call_target="tpu_custom_call" | custom-call | flops 3221225472 | bytes 11534336 | tf_op jit(solution)/shard_map/ladder/pallas_call | solution.py:26
  129.1 36.2 %all-to-all-done.1 = bf16[32,6,8,512]{3,2,1,0:T(8,128)(2,1)} async-done(((bf16[32,6,8,512]{3,2,1,0:T(8,128)(2,1)}), bf16[32,6,8,512]{3,2,1,0:T(8,128)(2,1)}, u32[]{:S(2)}, u32[]{:S(2)}) %all-to-all-start.1) | async-done | bytes 1572896 | tf_op jit(solution)/shard_map/all_to_all | solution.py:81
  165.3 3.1 %fusion = bf16[6,256,512]{2,1,0:T(8,128)(2,1)} fusion(f32[6,256,512]{2,1,0:T(8,128)S(1)} %bitcast.24, bf16[32,6,8,512]{3,2,1,0:T(8,128)(2,1)} %all-to-all-done.1), kind=kLoop, calls=%fused_computation.2 | loop fusion | flops 2359296 | bytes 6291456 | tf_op jit(solution)/shard_map/convert_element_type | solution.py:93
  (18 shorter events, 0.1 us)
Async XLA Ops:
  0.0 85.8 %copy-start = (bf16[192,192]{1,0:T(8,128)(2,1)S(1)}, bf16[192,192]{1,0:T(8,128)(2,1)}, u32[]{:S(2)}) copy-start(bf16[192,192]{1,0:T(8,128)(2,1)} %param.7) | copy-start | bytes 221188
  2.8 17.6 %copy-start.1 = (bf16[6,256,512]{2,1,0:T(8,128)(2,1)S(1)}, bf16[6,256,512]{2,1,0:T(8,128)(2,1)}, u32[]{:S(2)}) copy-start(bf16[6,256,512]{2,1,0:T(8,128)(2,1)} %param.4) | copy-start | bytes 4718596
  2.8 82.9 %all-to-all-start = ((bf16[32,6,8,512]{3,2,1,0:T(8,128)(2,1)}), bf16[32,6,8,512]{3,2,1,0:T(8,128)(2,1)}, u32[]{:S(2)}, u32[]{:S(2)}) async-start(bf16[32,6,8,512]{3,2,1,0:T(8,128)(2,1)} %copy.13), calls=%async_computation | async-start | bytes 3145728 | tf_op jit(solution)/shard_map/all_to_all | solution.py:70
  20.4 36.6 %collective-permute-start.1 = (bf16[6,256,512]{2,1,0:T(8,128)(2,1)S(1)}, bf16[6,256,512]{2,1,0:T(8,128)(2,1)S(1)}, u32[]{:S(2)}, u32[]{:S(2)}) collective-permute-start(bf16[6,256,512]{2,1,0:T(8,128)(2,1)S(1)} %copy-done.1), channel_id=1, source_target_pairs={{0,3},{1,0},{2,1},{3,2},{4,7},{5,4},{6,5},{7,6},{8,11},{9,8},{10,9... | collective-permute-start | bytes 4718600 | tf_op jit(solution)/shard_map/ppermute | solution.py:53
  22.6 36.4 %collective-permute-start = (bf16[6,256,512]{2,1,0:T(8,128)(2,1)S(1)}, bf16[6,256,512]{2,1,0:T(8,128)(2,1)}, u32[]{:S(2)}, u32[]{:S(2)}) collective-permute-start(bf16[6,256,512]{2,1,0:T(8,128)(2,1)S(1)} %copy-done.1), channel_id=1, source_target_pairs={{0,1},{1,2},{2,3},{3,0},{4,5},{5,6},{6,7},{7,4},{8,9},{9,10},{10,1... | collective-permute-start | bytes 4718600 | tf_op jit(solution)/shard_map/ppermute | solution.py:53
  57.1 40.5 %copy-start.3 = (bf16[6,256,512]{2,1,0:T(8,128)(2,1)}, bf16[6,256,512]{2,1,0:T(8,128)(2,1)S(1)}, u32[]{:S(2)}) copy-start(bf16[6,256,512]{2,1,0:T(8,128)(2,1)S(1)} %collective-permute-done.1) | copy-start | bytes 4718596
  90.4 74.9 %all-to-all-start.1 = ((bf16[32,6,8,512]{3,2,1,0:T(8,128)(2,1)}), bf16[32,6,8,512]{3,2,1,0:T(8,128)(2,1)}, u32[]{:S(2)}, u32[]{:S(2)}) async-start(bf16[32,6,8,512]{3,2,1,0:T(8,128)(2,1)} %bitcast.12), calls=%async_computation.1 | async-start | bytes 3145728 | tf_op jit(solution)/shard_map/all_to_all | solution.py:81
  95.5 8.3 %copy-start.9 = (s32[2048]{0:T(1024)S(1)}, s32[2048]{0:T(1024)}, u32[]{:S(2)}) copy-start(s32[2048]{0:T(1024)} %param.6) | copy-start | bytes 24580
  98.6 19.2 %collective-permute-start.3 = (bf16[3,256,512]{2,1,0:T(8,128)(2,1)}, bf16[3,256,512]{2,1,0:T(8,128)(2,1)S(1)}, u32[]{:S(2)}, u32[]{:S(2)}) collective-permute-start(bf16[3,256,512]{2,1,0:T(8,128)(2,1)} %slice.7), channel_id=1, source_target_pairs={{0,3},{1,0},{2,1},{3,2},{4,7},{5,4},{6,5},{7,6},{8,11},{9,8},{10,9... | collective-permute-start | bytes 2359304 | tf_op jit(solution)/shard_map/ppermute | solution.py:53
  100.7 18.9 %collective-permute-start.2 = (bf16[3,256,512]{2,1,0:T(8,128)(2,1)}, bf16[3,256,512]{2,1,0:T(8,128)(2,1)S(1)}, u32[]{:S(2)}, u32[]{:S(2)}) collective-permute-start(bf16[3,256,512]{2,1,0:T(8,128)(2,1)} %slice.6), channel_id=1, source_target_pairs={{0,1},{1,2},{2,3},{3,0},{4,5},{5,6},{6,7},{7,4},{8,9},{9,10},{10,1... | collective-permute-start | bytes 2359304 | tf_op jit(solution)/shard_map/ppermute | solution.py:53
  103.9 16.6 %copy-start.2 = (bf16[6,256,512]{2,1,0:T(8,128)(2,1)S(1)}, bf16[6,256,512]{2,1,0:T(8,128)(2,1)}, u32[]{:S(2)}) copy-start(bf16[6,256,512]{2,1,0:T(8,128)(2,1)} %param.4) | copy-start | bytes 4718596
  104.0 16.6 %copy-start.4 = (bf16[6,256,512]{2,1,0:T(8,128)(2,1)S(1)}, bf16[6,256,512]{2,1,0:T(8,128)(2,1)}, u32[]{:S(2)}) copy-start(bf16[6,256,512]{2,1,0:T(8,128)(2,1)} %copy-done.3) | copy-start | bytes 4718596
  117.8 0.9 copy-start.5
  119.7 0.9 copy-start.7
  120.6 1.1 copy-start.6
  121.7 1.1 copy-start.8

commit v4 on v3

--- a/solution.py
+++ b/solution.py
@@ -49,6 +49,39 @@
     )(order, own, below, above, far_low, far_high, masked)
 
 
+def spread_fock(occ_fock, copies):
+    size = occ_fock.shape[0]
+    spread = size * copies
+    wide = lax.broadcasted_iota(jnp.int32, (spread, size), 0) // copies
+    narrow = lax.broadcasted_iota(jnp.int32, (spread, size), 1)
+    expand = (wide == narrow).astype(jnp.bfloat16)
+    tall = jnp.dot(expand, -occ_fock, preferred_element_type=jnp.float32).astype(jnp.bfloat16)
+    full = jnp.dot(tall, expand.T, preferred_element_type=jnp.float32).astype(jnp.bfloat16)
+    row = lax.broadcasted_iota(jnp.int32, (spread, spread), 0) % copies
+    column = lax.broadcasted_iota(jnp.int32, (spread, spread), 1) % copies
+    return jnp.where(row == column, full, jnp.zeros_like(full))
+
+
+def add_kernel(ladder_ref, dressed_ref, out_ref):
+    dressed = dressed_ref[...].astype(jnp.float32).reshape(ladder_ref.shape)
+    out_ref[...] = (ladder_ref[...] + dressed).astype(out_ref.dtype)
+
+
+def add_dressed(ladder, dressed):
+    local_i, local_j, share = ladder.shape
+    rows, _, hub_j, _ = dressed.shape
+    whole = pl.BlockSpec((1, local_j, share), lambda i: (i, 0, 0))
+    return pl.pallas_call(
+        add_kernel,
+        grid=(local_i,),
+        in_specs=[whole, pl.BlockSpec((rows, 1, hub_j, share), lambda i: (0, i, 0, 0))],
+        out_specs=whole,
+        out_shape=jax.ShapeDtypeStruct(ladder.shape, jnp.bfloat16),
+        compiler_params=pltpu.CompilerParams(vmem_limit_bytes=16 * 1024 * 1024),
+        name="add_dressed",
+    )(ladder, dressed)
+
+
 def shift(block, depth, step):
     return lax.ppermute(block, "depth", [(d, (d + step) % depth) for d in range(depth)])
 
@@ -68,18 +101,17 @@
 
     blocks = amplitudes.reshape(local_i, rows, hub_j, share).transpose(1, 0, 2, 3)
     arrived = lax.all_to_all(blocks, "row", split_axis=0, concat_axis=0)
-    arrived, below, above = lax.optimization_barrier((arrived, below, above))
+    spread = spread_fock(occ_fock, hub_j)
+    arrived, below, above, spread = lax.optimization_barrier((arrived, below, above, spread))
     far_low = shift(below[: local_i // 2], depth, 1)
     far_high = shift(above[local_i // 2 :], depth, -1)
-    product = jnp.einsum(
-        "ik,kmn->imn",
-        occ_fock,
-        arrived.reshape(whole_i, hub_j, share),
+    product = jnp.dot(
+        spread,
+        arrived.reshape(whole_i * hub_j, share),
         preferred_element_type=jnp.float32,
     )
-    dressed_part = (-product).astype(jnp.bfloat16).reshape(rows, local_i, hub_j, share)
+    dressed_part = product.astype(jnp.bfloat16).reshape(rows, local_i, hub_j, share)
     dressed = lax.all_to_all(dressed_part, "row", split_axis=0, concat_axis=0)
-    dressed = dressed.transpose(1, 0, 2, 3).reshape(local_i, local_j, share)
 
     own_columns = lax.dynamic_slice(integrals, (0, offset), (whole_pairs, share))
     own_labels = lax.dynamic_slice_in_dim(pair_irreps, offset, share, 0)
@@ -90,7 +122,7 @@
         *(part.reshape(-1, share) for part in (amplitudes, below, above, far_low, far_high)),
         masked.reshape(depth, share, share),
     ).reshape(local_i, local_j, share)
-    return (ladder + dressed.astype(jnp.float32)).astype(jnp.bfloat16)
+    return add_dressed(ladder, dressed)
 
 
 def solution(mesh):

time: 169 us -> 172 us (1.018)
  the two profiles are of different devices: /device:TPU:141 before, /device:TPU:139 now
where the time goes in v4:
time: 172 us
  waiting for transfers between devices  105 us (61%)
  starting transfers between devices  33.2 us (19%)
  matrix products  12.5 us (7%)
  local copies, waits for them, and re-layouts  9.58 us (6%)
  Pallas kernels  9.12 us (5%)
  other arithmetic  2.03 us (1%)
    ppermute x4, waiting for transfers between devices, shift(): lax.ppermute(block, 'depth', [(d, (d + step) % depth) for d in range(dept...  43.6 us
    all_to_all x1, waiting for transfers between devices, on_device(): dressed = lax.all_to_all(dressed_part, 'row', split_axis=0, concat_axis=0)  36.2 us
    all_to_all x1, waiting for transfers between devices, on_device(): arrived = lax.all_to_all(blocks, 'row', split_axis=0, concat_axis=0)  25.5 us
    all_to_all x1, starting transfers between devices, on_device(): arrived = lax.all_to_all(blocks, 'row', split_axis=0, concat_axis=0)  17.6 us
    ppermute x4, starting transfers between devices, shift(): lax.ppermute(block, 'depth', [(d, (d + step) % depth) for d in range(dept...  10.6 us
    pallas_call x1, Pallas kernels, ladder_product(): pl.pallas_call(ladder_kernel, grid_spec=pltpu.PrefetchScalarGridSpec(num_...  6.7 us
    dot_general x1, matrix products, on_device(): jnp.dot(spread, arrived.reshape(whole_i * hub_j, share), preferred_elemen...  6.66 us
    dot_general x1, matrix products, spread_fock(): jnp.dot(tall, expand.T, preferred_element_type=jnp.float32)  5.88 us
  transfers between devices with their start and end apart: 6, of which 6 were waited for; matrix products, arithmetic and copies ran while one was open for 6% of the time, Pallas kernels for 4%

profile of v4, /device:TPU:139, one launch (start us, length us, event | category | flops | bytes accessed | tf_op | source)
XLA Modules:
  0.0 171.8 jit_solution(9015456869212754974)
XLA Ops:
  0.0 2.8 %copy.6 = bf16[32,6,8,512]{3,2,1,0:T(8,128)(2,1)} copy(bf16[32,6,8,512]{3,2,0,1:T(8,128)(2,1)} %bitcast.16) | data formatting | bytes 3145728 | tf_op jit(solution)/shard_map/transpose | solution.py:102
  2.8 17.6 %all-to-all-start = ((bf16[32,6,8,512]{3,2,1,0:T(8,128)(2,1)}), bf16[32,6,8,512]{3,2,1,0:T(8,128)(2,1)}, u32[]{:S(2)}, u32[]{:S(2)}) async-start(bf16[32,6,8,512]{3,2,1,0:T(8,128)(2,1)} %copy.6), calls=%async_computation | async-start | bytes 3145728 | tf_op jit(solution)/shard_map/all_to_all | solution.py:103
  20.5 2.2 %collective-permute-start.1 = (bf16[6,256,512]{2,1,0:T(8,128)(2,1)S(1)}, bf16[6,256,512]{2,1,0:T(8,128)(2,1)S(1)}, u32[]{:S(2)}, u32[]{:S(2)}) collective-permute-start(bf16[6,256,512]{2,1,0:T(8,128)(2,1)S(1)} %copy-done.2), channel_id=1, source_target_pairs={{0,3},{1,0},{2,1},{3,2},{4,7},{5,4},{6,5},{7,6},{8,11},{9,8},{10,9... | collective-permute-start | bytes 4718600 | tf_op jit(solution)/shard_map/ppermute | solution.py:86
  22.6 3.1 %collective-permute-start = (bf16[6,256,512]{2,1,0:T(8,128)(2,1)S(1)}, bf16[6,256,512]{2,1,0:T(8,128)(2,1)}, u32[]{:S(2)}, u32[]{:S(2)}) collective-permute-start(bf16[6,256,512]{2,1,0:T(8,128)(2,1)S(1)} %copy-done.2), channel_id=1, source_target_pairs={{0,1},{1,2},{2,3},{3,0},{4,5},{5,6},{6,7},{7,4},{8,9},{9,10},{10,1... | collective-permute-start | bytes 4718600 | tf_op jit(solution)/shard_map/ppermute | solution.py:86
  25.8 5.9 %fusion = bf16[1536,1536]{1,0:T(8,128)(2,1)} fusion(s32[1536]{0:T(1024)S(1)} %get-tuple-element.14, s32[1536]{0:T(1024)S(1)} %get-tuple-element.15, pred[1536]{0:T(1024)(128)(4,1)S(1)} %get-tuple-element.18, s32[1536]{0:T(1024)S(1)} %get-tuple-element.13, s32[1536]{0:T(1024)S(1)} %get-tuple-element.16, pred[1536]{0:T(1024)(128)(4,1)S(1)} %get-tuple-element.17, ...), kind=kOutput, calls=%fused_computation.1 | convolution fusion | flops 1032523776 | bytes 4819968 | tf_op jit(solution)/shard_map/dot_general | solution.py:59
  31.7 25.4 %collective-permute-done.1 = bf16[6,256,512]{2,1,0:T(8,128)(2,1)S(1)} collective-permute-done((bf16[6,256,512]{2,1,0:T(8,128)(2,1)S(1)}, bf16[6,256,512]{2,1,0:T(8,128)(2,1)S(1)}, u32[]{:S(2)}, u32[]{:S(2)}) %collective-permute-start.1) | collective-permute-done | bytes 1572896 | tf_op jit(solution)/shard_map/ppermute | solution.py:86
  57.1 3.2 %collective-permute-done = bf16[6,256,512]{2,1,0:T(8,128)(2,1)} collective-permute-done((bf16[6,256,512]{2,1,0:T(8,128)(2,1)S(1)}, bf16[6,256,512]{2,1,0:T(8,128)(2,1)}, u32[]{:S(2)}, u32[]{:S(2)}) %collective-permute-start) | collective-permute-done | bytes 1572896 | tf_op jit(solution)/shard_map/ppermute | solution.py:86
  60.3 25.5 %all-to-all-done = bf16[32,6,8,512]{3,2,1,0:T(8,128)(2,1)} async-done(((bf16[32,6,8,512]{3,2,1,0:T(8,128)(2,1)}), bf16[32,6,8,512]{3,2,1,0:T(8,128)(2,1)}, u32[]{:S(2)}, u32[]{:S(2)}) %all-to-all-start) | async-done | bytes 1572896 | tf_op jit(solution)/shard_map/all_to_all | solution.py:103
  85.8 6.7 %convolution_convert_fusion.1 = bf16[1536,512]{1,0:T(8,128)(2,1)} fusion(bf16[1536,1536]{1,0:T(8,128)(2,1)} %fusion, bf16[1536,512]{1,0:T(8,128)(2,1)} %bitcast.9), kind=kOutput, calls=%fused_computation.4 | convolution fusion | flops 2416705536 | bytes 7864320 | tf_op jit(solution)/shard_map/dot_general | solution.py:108
  92.4 5.0 %all-to-all-start.1 = ((bf16[32,6,8,512]{3,2,1,0:T(8,128)(2,1)}), bf16[32,6,8,512]{3,2,1,0:T(8,128)(2,1)S(1)}, u32[]{:S(2)}, u32[]{:S(2)}) async-start(bf16[32,6,8,512]{3,2,1,0:T(8,128)(2,1)} %bitcast.19), calls=%async_computation.1 | async-start | bytes 3145728 | tf_op jit(solution)/shard_map/all_to_all | solution.py:114
  97.5 0.0 copy-start.6
  97.5 2.2 %slice.6 = bf16[3,256,512]{2,1,0:T(8,128)(2,1)} slice(bf16[6,256,512]{2,1,0:T(8,128)(2,1)} %collective-permute-done), slice={[0:3], [0:256], [0:512]} | slice | bytes 1572864 | tf_op jit(solution)/shard_map/slice | solution.py:106
  99.7 0.9 slice.7
  100.6 2.2 %collective-permute-start.3 = (bf16[3,256,512]{2,1,0:T(8,128)(2,1)}, bf16[3,256,512]{2,1,0:T(8,128)(2,1)}, u32[]{:S(2)}, u32[]{:S(2)}) collective-permute-start(bf16[3,256,512]{2,1,0:T(8,128)(2,1)} %slice.7), channel_id=1, source_target_pairs={{0,3},{1,0},{2,1},{3,2},{4,7},{5,4},{6,5},{7,6},{8,11},{9,8},{10,9... | collective-permute-start | bytes 2359304 | tf_op jit(solution)/shard_map/ppermute | solution.py:86
  102.8 3.1 %collective-permute-start.2 = (bf16[3,256,512]{2,1,0:T(8,128)(2,1)}, bf16[3,256,512]{2,1,0:T(8,128)(2,1)}, u32[]{:S(2)}, u32[]{:S(2)}) collective-permute-start(bf16[3,256,512]{2,1,0:T(8,128)(2,1)} %slice.6), channel_id=1, source_target_pairs={{0,1},{1,2},{2,3},{3,0},{4,5},{5,6},{6,7},{7,4},{8,9},{9,10},{10,1... | collective-permute-start | bytes 2359304 | tf_op jit(solution)/shard_map/ppermute | solution.py:86
  105.9 0.1 dynamic_slice.6
  106.0 2.0 %compare_select_fusion = bf16[2048,512]{1,0:T(8,128)(2,1)S(1)} fusion(bf16[2048,2048]{1,0:T(8,128)(2,1)} %param.5, s32[]{:T(128)S(6)} %select_n.41, s32[512]{0:T(512)S(1)} %dynamic_slice.6, s32[2048]{0:T(1024)S(1)} %copy-done.6), kind=kLoop, calls=%fused_computation.3 | loop fusion | flops 2097152 | bytes 4204548 | tf_op jit(solution)/shard_map/jit(_where)/select_n | solution.py:119
  108.0 11.8 %collective-permute-done.3 = bf16[3,256,512]{2,1,0:T(8,128)(2,1)} collective-permute-done((bf16[3,256,512]{2,1,0:T(8,128)(2,1)}, bf16[3,256,512]{2,1,0:T(8,128)(2,1)}, u32[]{:S(2)}, u32[]{:S(2)}) %collective-permute-start.3) | collective-permute-done | bytes 786464 | tf_op jit(solution)/shard_map/ppermute | solution.py:86
  119.8 3.2 %collective-permute-done.2 = bf16[3,256,512]{2,1,0:T(8,128)(2,1)} collective-permute-done((bf16[3,256,512]{2,1,0:T(8,128)(2,1)}, bf16[3,256,512]{2,1,0:T(8,128)(2,1)}, u32[]{:S(2)}, u32[]{:S(2)}) %collective-permute-start.2) | collective-permute-done | bytes 786464 | tf_op jit(solution)/shard_map/ppermute | solution.py:86
  123.0 6.7 %ladder.1 = f32[1536,512]{1,0:T(8,128)S(1)} custom-call(s32[4]{0:T(128)S(1)} %and_select_fusion.order_ref, bf16[1536,512]{1,0:T(8,128)(2,1)S(1)} %bitcast.17, bf16[1536,512]{1,0:T(8,128)(2,1)} %bitcast.3.below_ref, bf16[1536,512]{1,0:T(8,128)(2,1)S(1)} %bitcast.18, bf16[768,512]{1,0:T(8,128)(2,1)} %bitcast.5.far_low_ref, ...), custom_call_target="tpu_custom_call" | custom-call | flops 3221225472 | bytes 11534336 | tf_op jit(solution)/shard_map/ladder/pallas_call | solution.py:26
  129.7 1.6 copy-done
  131.4 36.2 %all-to-all-done.1.dressed_ref = bf16[32,6,8,512]{3,2,1,0:T(8,128)(2,1)S(1)} async-done(((bf16[32,6,8,512]{3,2,1,0:T(8,128)(2,1)}), bf16[32,6,8,512]{3,2,1,0:T(8,128)(2,1)S(1)}, u32[]{:S(2)}, u32[]{:S(2)}) %all-to-all-start.1) | async-done | bytes 1572896 | tf_op jit(solution)/shard_map/all_to_all | solution.py:114
  167.5 1.9 %copy-done.1 = f32[1536,512]{1,0:T(8,128)S(1)} copy-done((f32[1536,512]{1,0:T(8,128)S(1)}, f32[1536,512]{1,0:T(8,128)}, u32[]{:S(2)}) %copy-start.1) | copy-done | bytes 3145752
  169.4 2.4 %add_dressed.1 = bf16[6,256,512]{2,1,0:T(8,128)(2,1)} custom-call(f32[6,256,512]{2,1,0:T(8,128)S(1)} %bitcast.14, bf16[32,6,8,512]{3,2,1,0:T(8,128)(2,1)S(1)} %all-to-all-done.1.dressed_ref), custom_call_target="tpu_custom_call" | custom-call | tf_op jit(solution)/shard_map/add_dressed/pallas_call | solution.py:74
  (17 shorter events, 0.1 us)
Async XLA Ops:
  2.8 17.6 %copy-start.2 = (bf16[6,256,512]{2,1,0:T(8,128)(2,1)S(1)}, bf16[6,256,512]{2,1,0:T(8,128)(2,1)}, u32[]{:S(2)}) copy-start(bf16[6,256,512]{2,1,0:T(8,128)(2,1)} %param.4) | copy-start | bytes 4718596
  2.8 23.0 %copy-start.7 = (bf16[192,192]{1,0:T(8,128)(2,1)S(1)}, bf16[192,192]{1,0:T(8,128)(2,1)}, u32[]{:S(2)}) copy-start(bf16[192,192]{1,0:T(8,128)(2,1)} %param.7) | copy-start | bytes 221188
  2.8 82.9 %all-to-all-start = ((bf16[32,6,8,512]{3,2,1,0:T(8,128)(2,1)}), bf16[32,6,8,512]{3,2,1,0:T(8,128)(2,1)}, u32[]{:S(2)}, u32[]{:S(2)}) async-start(bf16[32,6,8,512]{3,2,1,0:T(8,128)(2,1)} %copy.6), calls=%async_computation | async-start | bytes 3145728 | tf_op jit(solution)/shard_map/all_to_all | solution.py:103
  20.5 36.6 %collective-permute-start.1 = (bf16[6,256,512]{2,1,0:T(8,128)(2,1)S(1)}, bf16[6,256,512]{2,1,0:T(8,128)(2,1)S(1)}, u32[]{:S(2)}, u32[]{:S(2)}) collective-permute-start(bf16[6,256,512]{2,1,0:T(8,128)(2,1)S(1)} %copy-done.2), channel_id=1, source_target_pairs={{0,3},{1,0},{2,1},{3,2},{4,7},{5,4},{6,5},{7,6},{8,11},{9,8},{10,9... | collective-permute-start | bytes 4718600 | tf_op jit(solution)/shard_map/ppermute | solution.py:86
  22.6 37.7 %collective-permute-start = (bf16[6,256,512]{2,1,0:T(8,128)(2,1)S(1)}, bf16[6,256,512]{2,1,0:T(8,128)(2,1)}, u32[]{:S(2)}, u32[]{:S(2)}) collective-permute-start(bf16[6,256,512]{2,1,0:T(8,128)(2,1)S(1)} %copy-done.2), channel_id=1, source_target_pairs={{0,1},{1,2},{2,3},{3,0},{4,5},{5,6},{6,7},{7,4},{8,9},{9,10},{10,1... | collective-permute-start | bytes 4718600 | tf_op jit(solution)/shard_map/ppermute | solution.py:86
  57.1 35.3 %copy-start.3 = (bf16[6,256,512]{2,1,0:T(8,128)(2,1)}, bf16[6,256,512]{2,1,0:T(8,128)(2,1)S(1)}, u32[]{:S(2)}) copy-start(bf16[6,256,512]{2,1,0:T(8,128)(2,1)S(1)} %collective-permute-done.1) | copy-start | bytes 4718596
  92.4 75.1 %all-to-all-start.1 = ((bf16[32,6,8,512]{3,2,1,0:T(8,128)(2,1)}), bf16[32,6,8,512]{3,2,1,0:T(8,128)(2,1)S(1)}, u32[]{:S(2)}, u32[]{:S(2)}) async-start(bf16[32,6,8,512]{3,2,1,0:T(8,128)(2,1)} %bitcast.19), calls=%async_computation.1 | async-start | bytes 3145728 | tf_op jit(solution)/shard_map/all_to_all | solution.py:114
  97.4 2.2 %copy-start.4 = (bf16[6,256,512]{2,1,0:T(8,128)(2,1)S(1)}, bf16[6,256,512]{2,1,0:T(8,128)(2,1)}, u32[]{:S(2)}) copy-start(bf16[6,256,512]{2,1,0:T(8,128)(2,1)} %copy-done.3) | copy-start | bytes 4718596
  97.5 8.4 %copy-start.6 = (s32[2048]{0:T(1024)S(1)}, s32[2048]{0:T(1024)}, u32[]{:S(2)}) copy-start(s32[2048]{0:T(1024)} %param.6) | copy-start | bytes 24580
  100.6 19.2 %collective-permute-start.3 = (bf16[3,256,512]{2,1,0:T(8,128)(2,1)}, bf16[3,256,512]{2,1,0:T(8,128)(2,1)}, u32[]{:S(2)}, u32[]{:S(2)}) collective-permute-start(bf16[3,256,512]{2,1,0:T(8,128)(2,1)} %slice.7), channel_id=1, source_target_pairs={{0,3},{1,0},{2,1},{3,2},{4,7},{5,4},{6,5},{7,6},{8,11},{9,8},{10,9... | collective-permute-start | bytes 2359304 | tf_op jit(solution)/shard_map/ppermute | solution.py:86
  102.8 20.2 %collective-permute-start.2 = (bf16[3,256,512]{2,1,0:T(8,128)(2,1)}, bf16[3,256,512]{2,1,0:T(8,128)(2,1)}, u32[]{:S(2)}, u32[]{:S(2)}) collective-permute-start(bf16[3,256,512]{2,1,0:T(8,128)(2,1)} %slice.6), channel_id=1, source_target_pairs={{0,1},{1,2},{2,3},{3,0},{4,5},{5,6},{6,7},{7,4},{8,9},{9,10},{10,1... | collective-permute-start | bytes 2359304 | tf_op jit(solution)/shard_map/ppermute | solution.py:86
  106.0 17.0 %copy-start.5 = (bf16[6,256,512]{2,1,0:T(8,128)(2,1)S(1)}, bf16[6,256,512]{2,1,0:T(8,128)(2,1)}, u32[]{:S(2)}) copy-start(bf16[6,256,512]{2,1,0:T(8,128)(2,1)} %copy-done.3) | copy-start | bytes 4718596
  129.7 1.6 copy-start
  167.5 1.9 %copy-start.1 = (f32[1536,512]{1,0:T(8,128)S(1)}, f32[1536,512]{1,0:T(8,128)}, u32[]{:S(2)}) copy-start(f32[1536,512]{1,0:T(8,128)} %copy-done) | copy-start | bytes 9437188

commit v5 on v3

--- a/solution.py
+++ b/solution.py
@@ -68,19 +68,8 @@
 
     blocks = amplitudes.reshape(local_i, rows, hub_j, share).transpose(1, 0, 2, 3)
     arrived = lax.all_to_all(blocks, "row", split_axis=0, concat_axis=0)
-    arrived, below, above = lax.optimization_barrier((arrived, below, above))
     far_low = shift(below[: local_i // 2], depth, 1)
     far_high = shift(above[local_i // 2 :], depth, -1)
-    product = jnp.einsum(
-        "ik,kmn->imn",
-        occ_fock,
-        arrived.reshape(whole_i, hub_j, share),
-        preferred_element_type=jnp.float32,
-    )
-    dressed_part = (-product).astype(jnp.bfloat16).reshape(rows, local_i, hub_j, share)
-    dressed = lax.all_to_all(dressed_part, "row", split_axis=0, concat_axis=0)
-    dressed = dressed.transpose(1, 0, 2, 3).reshape(local_i, local_j, share)
-
     own_columns = lax.dynamic_slice(integrals, (0, offset), (whole_pairs, share))
     own_labels = lax.dynamic_slice_in_dim(pair_irreps, offset, share, 0)
     same = pair_irreps[:, None] == own_labels[None, :]
@@ -90,6 +79,16 @@
         *(part.reshape(-1, share) for part in (amplitudes, below, above, far_low, far_high)),
         masked.reshape(depth, share, share),
     ).reshape(local_i, local_j, share)
+    tied_fock, ladder = lax.optimization_barrier((occ_fock, ladder))
+    product = jnp.einsum(
+        "ik,kmn->imn",
+        tied_fock,
+        arrived.reshape(whole_i, hub_j, share),
+        preferred_element_type=jnp.float32,
+    )
+    dressed_part = (-product).astype(jnp.bfloat16).reshape(rows, local_i, hub_j, share)
+    dressed = lax.all_to_all(dressed_part, "row", split_axis=0, concat_axis=0)
+    dressed = dressed.transpose(1, 0, 2, 3).reshape(local_i, local_j, share)
     return (ladder + dressed.astype(jnp.float32)).astype(jnp.bfloat16)
 
 

time: 169 us -> 173 us (1.024)
  the two profiles are of different devices: /device:TPU:141 before, /device:TPU:78 now
where the time goes in v5:
time: 173 us
  blocking collectives  72.4 us (42%)
  waiting for transfers between devices  47.9 us (28%)
  starting transfers between devices  31.3 us (18%)
  local copies, waits for them, and re-layouts  8.24 us (5%)
  Pallas kernels  6.05 us (3%)
  other arithmetic  3.83 us (2%)
  matrix products  2.66 us (2%)
    all_to_all x1, blocking collectives, on_device(): dressed = lax.all_to_all(dressed_part, 'row', split_axis=0, concat_axis=0)  72.4 us
    ppermute x4, waiting for transfers between devices, shift(): lax.ppermute(block, 'depth', [(d, (d + step) % depth) for d in range(dept...  47.9 us
    all_to_all x1, starting transfers between devices, on_device(): arrived = lax.all_to_all(blocks, 'row', split_axis=0, concat_axis=0)  19.6 us
    ppermute x4, starting transfers between devices, shift(): lax.ppermute(block, 'depth', [(d, (d + step) % depth) for d in range(dept...  11.7 us
    pallas_call x1, Pallas kernels, ladder_product(): pl.pallas_call(ladder_kernel, grid_spec=pltpu.PrefetchScalarGridSpec(num_...  6.05 us
  transfers between devices with their start and end apart: 5, of which 3 were waited for; matrix products, arithmetic and copies ran while one was open for 2% of the time, Pallas kernels for 4%

profile of v5, /device:TPU:78, one launch (start us, length us, event | category | flops | bytes accessed | tf_op | source)
XLA Modules:
  0.0 172.6 jit_solution(6946455324648072453)
XLA Ops:
  0.0 2.8 %copy.13 = bf16[32,6,8,512]{3,2,1,0:T(8,128)(2,1)} copy(bf16[32,6,8,512]{3,2,0,1:T(8,128)(2,1)} %bitcast.24) | data formatting | bytes 3145728 | tf_op jit(solution)/shard_map/transpose | solution.py:69
  2.8 19.6 %all-to-all-start = ((bf16[32,6,8,512]{3,2,1,0:T(8,128)(2,1)}), bf16[32,6,8,512]{3,2,1,0:T(8,128)(2,1)}, u32[]{:S(2)}, u32[]{:S(2)}) async-start(bf16[32,6,8,512]{3,2,1,0:T(8,128)(2,1)} %copy.13), calls=%async_computation | async-start | bytes 3145728 | tf_op jit(solution)/shard_map/all_to_all | solution.py:70
  22.5 0.0 copy-start.9
  22.5 2.4 %collective-permute-start = (bf16[6,256,512]{2,1,0:T(8,128)(2,1)S(1)}, bf16[6,256,512]{2,1,0:T(8,128)(2,1)S(1)}, u32[]{:S(2)}, u32[]{:S(2)}) collective-permute-start(bf16[6,256,512]{2,1,0:T(8,128)(2,1)S(1)} %copy-done.1), channel_id=1, source_target_pairs={{0,1},{1,2},{2,3},{3,0},{4,5},{5,6},{6,7},{7,4},{8,9},{9,10},{10,1... | collective-permute-start | bytes 4718600 | tf_op jit(solution)/shard_map/ppermute | solution.py:53
  24.9 3.5 %collective-permute-start.1 = (bf16[6,256,512]{2,1,0:T(8,128)(2,1)S(1)}, bf16[6,256,512]{2,1,0:T(8,128)(2,1)S(1)}, u32[]{:S(2)}, u32[]{:S(2)}) collective-permute-start(bf16[6,256,512]{2,1,0:T(8,128)(2,1)S(1)} %copy-done.1), channel_id=1, source_target_pairs={{0,3},{1,0},{2,1},{3,2},{4,7},{5,4},{6,5},{7,6},{8,11},{9,8},{10,9... | collective-permute-start | bytes 4718600 | tf_op jit(solution)/shard_map/ppermute | solution.py:53
  28.3 31.6 %collective-permute-done = bf16[6,256,512]{2,1,0:T(8,128)(2,1)S(1)} collective-permute-done((bf16[6,256,512]{2,1,0:T(8,128)(2,1)S(1)}, bf16[6,256,512]{2,1,0:T(8,128)(2,1)S(1)}, u32[]{:S(2)}, u32[]{:S(2)}) %collective-permute-start) | collective-permute-done | bytes 1572896 | tf_op jit(solution)/shard_map/ppermute | solution.py:53
  59.9 1.0 slice.8
  60.9 3.6 %collective-permute-start.2 = (bf16[3,256,512]{2,1,0:T(8,128)(2,1)}, bf16[3,256,512]{2,1,0:T(8,128)(2,1)}, u32[]{:S(2)}, u32[]{:S(2)}) collective-permute-start(bf16[3,256,512]{2,1,0:T(8,128)(2,1)} %slice.8), channel_id=1, source_target_pairs={{0,1},{1,2},{2,3},{3,0},{4,5},{5,6},{6,7},{7,4},{8,9},{9,10},{10,1... | collective-permute-start | bytes 2359304 | tf_op jit(solution)/shard_map/ppermute | solution.py:53
  64.6 0.1 slice.9
  64.6 2.2 %collective-permute-start.3 = (bf16[3,256,512]{2,1,0:T(8,128)(2,1)S(1)}, bf16[3,256,512]{2,1,0:T(8,128)(2,1)S(1)}, u32[]{:S(2)}, u32[]{:S(2)}) collective-permute-start(bf16[3,256,512]{2,1,0:T(8,128)(2,1)S(1)} %slice.9), channel_id=1, source_target_pairs={{0,3},{1,0},{2,1},{3,2},{4,7},{5,4},{6,5},{7,6},{8,11},{9,8},{10,9... | collective-permute-start | bytes 2359304 | tf_op jit(solution)/shard_map/ppermute | solution.py:53
  66.9 0.1 dynamic_slice.6
  67.0 0.0 copy-start.4
  67.0 2.0 %compare_select_fusion = bf16[2048,512]{1,0:T(8,128)(2,1)S(1)} fusion(bf16[2048,2048]{1,0:T(8,128)(2,1)} %param.5, s32[]{:T(128)S(6)} %select_n.16, s32[512]{0:T(512)S(1)} %dynamic_slice.6, s32[2048]{0:T(1024)S(1)} %copy-done.9), kind=kLoop, calls=%fused_computation | loop fusion | flops 2097152 | bytes 4204548 | tf_op jit(solution)/shard_map/jit(_where)/select_n | solution.py:76
  69.1 12.0 %collective-permute-done.2 = bf16[3,256,512]{2,1,0:T(8,128)(2,1)} collective-permute-done((bf16[3,256,512]{2,1,0:T(8,128)(2,1)}, bf16[3,256,512]{2,1,0:T(8,128)(2,1)}, u32[]{:S(2)}, u32[]{:S(2)}) %collective-permute-start.2) | collective-permute-done | bytes 786464 | tf_op jit(solution)/shard_map/ppermute | solution.py:53
  81.0 4.3 %collective-permute-done.3 = bf16[3,256,512]{2,1,0:T(8,128)(2,1)S(1)} collective-permute-done((bf16[3,256,512]{2,1,0:T(8,128)(2,1)S(1)}, bf16[3,256,512]{2,1,0:T(8,128)(2,1)S(1)}, u32[]{:S(2)}, u32[]{:S(2)}) %collective-permute-start.3) | collective-permute-done | bytes 786464 | tf_op jit(solution)/shard_map/ppermute | solution.py:53
  85.4 0.9 copy-done.7
  86.2 1.4 copy-done.6
  87.7 1.1 copy-done.8
  88.8 6.0 %ladder.1 = f32[1536,512]{1,0:T(8,128)S(1)} custom-call(s32[4]{0:T(128)S(1)} %and_select_fusion.order_ref, bf16[1536,512]{1,0:T(8,128)(2,1)S(1)} %bitcast.25, bf16[1536,512]{1,0:T(8,128)(2,1)S(1)} %bitcast.26, bf16[1536,512]{1,0:T(8,128)(2,1)S(1)} %bitcast.27, bf16[768,512]{1,0:T(8,128)(2,1)} %bitcast.3.far_low_ref, bf16[768,512]{1,0:T(8,128)(2,1)S(1)} %bitcast.28, ...), custom_call_target="tpu_custom_call" | custom-call | flops 3221225472 | bytes 11534336 | tf_op jit(solution)/shard_map/ladder/pallas_call | solution.py:26
  94.8 0.0 all-to-all-done
  94.9 2.7 %negate_convert_fusion = bf16[192,8,512]{2,0,1:T(8,128)(2,1)S(1)} fusion(bf16[192,8,512]{2,1,0:T(8,128)(2,1)} %bitcast.10, bf16[192,192]{1,0:T(8,128)(2,1)S(1)} %copy-done), kind=kOutput, calls=%fused_computation.4 | convolution fusion | flops 303562752 | bytes 3219456 | tf_op jit(solution)/shard_map/ik,kmn->imn/dot_general | solution.py:83
  97.5 0.9 copy.15
  98.4 72.4 %all_to_all.10 = bf16[32,6,8,512]{3,2,1,0:T(8,128)(2,1)S(1)} all-to-all(bf16[32,6,8,512]{3,2,1,0:T(8,128)(2,1)S(1)} %bitcast.29), channel_id=1, replica_groups=mesh['row'=32,'col'=6,'depth'=4] {'row'}, dimensions={0} | all-to-all | bytes 3145728 | tf_op jit(solution)/shard_map/all_to_all | solution.py:90
  170.8 1.8 %fusion = bf16[6,256,512]{2,1,0:T(8,128)(2,1)} fusion(f32[6,256,512]{2,1,0:T(8,128)S(1)} %bitcast.22, bf16[32,6,8,512]{3,2,1,0:T(8,128)(2,1)S(1)} %all_to_all.10), kind=kLoop, calls=%fused_computation.2 | loop fusion | flops 2359296 | bytes 6291456 | tf_op jit(solution)/shard_map/convert_element_type | solution.py:92
  (17 shorter events, 0.0 us)
Async XLA Ops:
  0.0 94.8 %copy-start = (bf16[192,192]{1,0:T(8,128)(2,1)S(1)}, bf16[192,192]{1,0:T(8,128)(2,1)}, u32[]{:S(2)}) copy-start(bf16[192,192]{1,0:T(8,128)(2,1)} %param.7) | copy-start | bytes 221188
  2.8 19.7 %copy-start.1 = (bf16[6,256,512]{2,1,0:T(8,128)(2,1)S(1)}, bf16[6,256,512]{2,1,0:T(8,128)(2,1)}, u32[]{:S(2)}) copy-start(bf16[6,256,512]{2,1,0:T(8,128)(2,1)} %param.4) | copy-start | bytes 4718596
  2.8 92.0 %all-to-all-start = ((bf16[32,6,8,512]{3,2,1,0:T(8,128)(2,1)}), bf16[32,6,8,512]{3,2,1,0:T(8,128)(2,1)}, u32[]{:S(2)}, u32[]{:S(2)}) async-start(bf16[32,6,8,512]{3,2,1,0:T(8,128)(2,1)} %copy.13), calls=%async_computation | async-start | bytes 3145728 | tf_op jit(solution)/shard_map/all_to_all | solution.py:70
  22.5 44.4 %copy-start.9 = (s32[2048]{0:T(1024)S(1)}, s32[2048]{0:T(1024)}, u32[]{:S(2)}) copy-start(s32[2048]{0:T(1024)} %param.6) | copy-start | bytes 24580
  22.5 37.5 %collective-permute-start = (bf16[6,256,512]{2,1,0:T(8,128)(2,1)S(1)}, bf16[6,256,512]{2,1,0:T(8,128)(2,1)S(1)}, u32[]{:S(2)}, u32[]{:S(2)}) collective-permute-start(bf16[6,256,512]{2,1,0:T(8,128)(2,1)S(1)} %copy-done.1), channel_id=1, source_target_pairs={{0,1},{1,2},{2,3},{3,0},{4,5},{5,6},{6,7},{7,4},{8,9},{9,10},{10,1... | collective-permute-start | bytes 4718600 | tf_op jit(solution)/shard_map/ppermute | solution.py:53
  24.9 39.7 %collective-permute-start.1 = (bf16[6,256,512]{2,1,0:T(8,128)(2,1)S(1)}, bf16[6,256,512]{2,1,0:T(8,128)(2,1)S(1)}, u32[]{:S(2)}, u32[]{:S(2)}) collective-permute-start(bf16[6,256,512]{2,1,0:T(8,128)(2,1)S(1)} %copy-done.1), channel_id=1, source_target_pairs={{0,3},{1,0},{2,1},{3,2},{4,7},{5,4},{6,5},{7,6},{8,11},{9,8},{10,9... | collective-permute-start | bytes 4718600 | tf_op jit(solution)/shard_map/ppermute | solution.py:53
  59.9 4.7 %copy-start.3 = (bf16[6,256,512]{2,1,0:T(8,128)(2,1)}, bf16[6,256,512]{2,1,0:T(8,128)(2,1)S(1)}, u32[]{:S(2)}) copy-start(bf16[6,256,512]{2,1,0:T(8,128)(2,1)S(1)} %collective-permute-done) | copy-start | bytes 4718596
  60.9 20.1 %collective-permute-start.2 = (bf16[3,256,512]{2,1,0:T(8,128)(2,1)}, bf16[3,256,512]{2,1,0:T(8,128)(2,1)}, u32[]{:S(2)}, u32[]{:S(2)}) collective-permute-start(bf16[3,256,512]{2,1,0:T(8,128)(2,1)} %slice.8), channel_id=1, source_target_pairs={{0,1},{1,2},{2,3},{3,0},{4,5},{5,6},{6,7},{7,4},{8,9},{9,10},{10,1... | collective-permute-start | bytes 2359304 | tf_op jit(solution)/shard_map/ppermute | solution.py:53
  64.5 2.3 %copy-start.5 = (bf16[6,256,512]{2,1,0:T(8,128)(2,1)}, bf16[6,256,512]{2,1,0:T(8,128)(2,1)S(1)}, u32[]{:S(2)}) copy-start(bf16[6,256,512]{2,1,0:T(8,128)(2,1)S(1)} %collective-permute-done.1) | copy-start | bytes 4718596
  64.6 20.7 %collective-permute-start.3 = (bf16[3,256,512]{2,1,0:T(8,128)(2,1)S(1)}, bf16[3,256,512]{2,1,0:T(8,128)(2,1)S(1)}, u32[]{:S(2)}, u32[]{:S(2)}) collective-permute-start(bf16[3,256,512]{2,1,0:T(8,128)(2,1)S(1)} %slice.9), channel_id=1, source_target_pairs={{0,3},{1,0},{2,1},{3,2},{4,7},{5,4},{6,5},{7,6},{8,11},{9,8},{10,9... | collective-permute-start | bytes 2359304 | tf_op jit(solution)/shard_map/ppermute | solution.py:53
  67.0 19.2 %copy-start.2 = (bf16[6,256,512]{2,1,0:T(8,128)(2,1)S(1)}, bf16[6,256,512]{2,1,0:T(8,128)(2,1)}, u32[]{:S(2)}) copy-start(bf16[6,256,512]{2,1,0:T(8,128)(2,1)} %param.4) | copy-start | bytes 4718596
  67.0 19.2 %copy-start.4 = (bf16[6,256,512]{2,1,0:T(8,128)(2,1)S(1)}, bf16[6,256,512]{2,1,0:T(8,128)(2,1)}, u32[]{:S(2)}) copy-start(bf16[6,256,512]{2,1,0:T(8,128)(2,1)} %copy-done.3) | copy-start | bytes 4718596
  85.4 0.9 copy-start.7
  86.2 1.4 copy-start.6
  87.7 1.1 copy-start.8

commit v6 on v2

v6 whole, which is shorter than its diff:
```python
import jax
import jax.numpy as jnp
from jax import lax
from jax.experimental import pallas as pl
from jax.experimental.pallas import tpu as pltpu
from jax.sharding import PartitionSpec as P


def ladder_kernel(from_ref, to_ref, *refs):
    part_refs, masked_ref, out_ref = refs[:-2], refs[-2], refs[-1]
    share = part_refs[0].shape[1]
    total = None
    for s, part_ref in enumerate(part_refs):
        start = pl.multiple_of(from_ref[s] * share, share)
        term = jnp.dot(
            part_ref[...], masked_ref[pl.ds(start, share), :], preferred_element_type=jnp.float32
        )
        total = term if total is None else total + term
    out_ref[0] = total.astype(out_ref.dtype)


def ladder_product(came_from, goes_to, parts, masked):
    depth = len(parts)
    rows, share = parts[0].shape
    whole_pairs = masked.shape[0]
    return pl.pallas_call(
        ladder_kernel,
        grid_spec=pltpu.PrefetchScalarGridSpec(
            num_scalar_prefetch=2,
            grid=(depth,),
            in_specs=[pl.BlockSpec((rows, share), lambda t, came, goes: (0, 0))] * depth
            + [pl.BlockSpec((whole_pairs, share), lambda t, came, goes: (0, goes[t]))],
            out_specs=pl.BlockSpec((1, rows, share), lambda t, came, goes: (t, 0, 0)),
        ),
        out_shape=jax.ShapeDtypeStruct((depth, rows, share), jnp.bfloat16),
        compiler_params=pltpu.CompilerParams(vmem_limit_bytes=24 * 1024 * 1024),
        cost_estimate=pl.CostEstimate(
            flops=2 * rows * whole_pairs * whole_pairs,
            bytes_accessed=2 * whole_pairs * whole_pairs + 4 * depth * rows * share,
            transcendentals=0,
        ),
        name="ladder",
    )(came_from, goes_to, *parts, masked)


def shift(block, depth, step):
    return lax.ppermute(block, "depth", [(d, (d + step) % depth) for d in range(depth)])


def on_device(amplitudes, integrals, pair_irreps, occ_fock):
    local_i, local_j, share = amplitudes.shape
    whole_pairs = integrals.shape[0]
    whole_i = occ_fock.shape[0]
    rows = whole_i // local_i
    depth = whole_pairs // share
    hub_j = local_j // rows
    part_j = local_j // depth
    here = lax.axis_index("depth")
    steps = jnp.arange(depth, dtype=jnp.int32)
    came_from = (here - steps + depth) % depth
    goes_to = (here + steps) % depth

    blocks = amplitudes.reshape(local_i, rows, hub_j, share).transpose(1, 0, 2, 3)
    arrived = lax.all_to_all(blocks, "row", split_axis=0, concat_axis=0)

    parts = []
    for s in range(depth):
        start = ((here + s) % depth) * part_j
        part = lax.dynamic_slice(amplitudes, (0, start, 0), (local_i, part_j, share))
        parts.append(part if s == 0 else shift(part, depth, s))
    same = pair_irreps[:, None] == pair_irreps[None, :]
    masked = jnp.where(same, integrals, jnp.zeros_like(integrals))
    columns = ladder_product(
        came_from, goes_to, [part.reshape(local_i * part_j, share) for part in parts], masked
    ).reshape(depth, local_i, part_j, share)
    ladder = jnp.zeros_like(amplitudes)
    for t in range(depth):
        piece = columns[0] if t == 0 else shift(columns[t], depth, t)
        start = ((here - t + depth) % depth) * part_j
        ladder = lax.dynamic_update_slice(ladder, piece, (0, start, 0))

    tied_fock, ladder = lax.optimization_barrier((occ_fock, ladder))
    product = jnp.einsum(
        "ik,kmn->imn",
        tied_fock,
        arrived.reshape(whole_i, hub_j, share),
        preferred_element_type=jnp.float32,
    )
    dressed_part = (-product).astype(jnp.bfloat16).reshape(rows, local_i, hub_j, share)
    dressed = lax.all_to_all(dressed_part, "row", split_axis=0, concat_axis=0)
    dressed = dressed.transpose(1, 0, 2, 3).reshape(local_i, local_j, share)
    return (ladder.astype(jnp.float32) + dressed.astype(jnp.float32)).astype(jnp.bfloat16)


def solution(mesh):
    placed = (P("row", "col", "depth"), P(), P(), P())
    return jax.shard_map(
        on_device, mesh=mesh, in_specs=placed, out_specs=P("row", "col", "depth"), check_vma=False
    )
```

time: 180 us -> 161 us (0.89)
  the two profiles are of different devices: /device:TPU:67 before, /device:TPU:10 now
where the time goes in v6:
time: 161 us; the launch traced here: 160 us
  blocking collectives  75 us (47%)
  starting transfers between devices  40.4 us (25%)
  waiting for transfers between devices  21.9 us (14%)
  local copies, waits for them, and re-layouts  9.06 us (6%)
  other arithmetic  6.92 us (4%)
  Pallas kernels  5.18 us (3%)
    all_to_all x1, blocking collectives, on_device(): dressed = lax.all_to_all(dressed_part, 'row', split_axis=0, concat_axis=0)  75 us
    ppermute x6, waiting for transfers between devices, shift(): lax.ppermute(block, 'depth', [(d, (d + step) % depth) for d in range(dept...  21.9 us
    all_to_all x1, starting transfers between devices, on_device(): arrived = lax.all_to_all(blocks, 'row', split_axis=0, concat_axis=0)  20.5 us
    ppermute x6, starting transfers between devices, shift(): lax.ppermute(block, 'depth', [(d, (d + step) % depth) for d in range(dept...  19.9 us
    select_n x1, other arithmetic, on_device(): masked = jnp.where(same, integrals, jnp.zeros_like(integrals))  5.32 us
    pallas_call x1, Pallas kernels, ladder_product(): pl.pallas_call(ladder_kernel, grid_spec=pltpu.PrefetchScalarGridSpec(num_...  5.18 us
  transfers between devices with their start and end apart: 7, of which 5 were waited for; matrix products, arithmetic and copies ran while one was open for 6% of the time, Pallas kernels for 3%

profile of v6, /device:TPU:10, one launch (start us, length us, event | category | flops | bytes accessed | tf_op | source)
XLA Modules:
  0.0 160.0 jit_solution(8540443435600567373)
XLA Ops:
  0.0 2.8 %copy.13 = bf16[32,6,8,512]{3,2,1,0:T(8,128)(2,1)} copy(bf16[32,6,8,512]{3,2,0,1:T(8,128)(2,1)} %bitcast.28) | data formatting | bytes 3145728 | tf_op jit(solution)/shard_map/transpose | solution.py:63
  2.8 20.5 %all-to-all-start = ((bf16[32,6,8,512]{3,2,1,0:T(8,128)(2,1)}), bf16[32,6,8,512]{3,2,1,0:T(8,128)(2,1)S(1)}, u32[]{:S(2)}, u32[]{:S(2)}) async-start(bf16[32,6,8,512]{3,2,1,0:T(8,128)(2,1)} %copy.13), calls=%async_computation | async-start | bytes 3145728 | tf_op jit(solution)/shard_map/all_to_all | solution.py:64
  23.5 3.4 %collective-permute-start = (bf16[6,64,512]{2,1,0:T(8,128)(2,1)S(1)}, bf16[6,64,512]{2,1,0:T(8,128)(2,1)S(1)}, u32[]{:S(2)}, u32[]{:S(2)}) collective-permute-start(bf16[6,64,512]{2,1,0:T(8,128)(2,1)S(1)} %get-tuple-element.15), channel_id=1, source_target_pairs={{0,1},{1,2},{2,3},{3,0},{4,5},{5,6},{6,7},{7,4},{8,9},{9,10},{10,1... | collective-permute-start | bytes 1179656 | tf_op jit(solution)/shard_map/ppermute | solution.py:47
  26.9 3.0 %collective-permute-start.1 = (bf16[6,64,512]{2,1,0:T(8,128)(2,1)S(1)}, bf16[6,64,512]{2,1,0:T(8,128)(2,1)S(1)}, u32[]{:S(2)}, u32[]{:S(2)}) collective-permute-start(bf16[6,64,512]{2,1,0:T(8,128)(2,1)S(1)} %get-tuple-element.14), channel_id=1, source_target_pairs={{0,2},{1,3},{2,0},{3,1},{4,6},{5,7},{6,4},{7,5},{8,10},{9,11},{10,... | collective-permute-start | bytes 1179656 | tf_op jit(solution)/shard_map/ppermute | solution.py:47
  29.9 4.1 %collective-permute-start.2 = (bf16[6,64,512]{2,1,0:T(8,128)(2,1)S(1)}, bf16[6,64,512]{2,1,0:T(8,128)(2,1)S(1)}, u32[]{:S(2)}, u32[]{:S(2)}) collective-permute-start(bf16[6,64,512]{2,1,0:T(8,128)(2,1)S(1)} %get-tuple-element.13), channel_id=1, source_target_pairs={{0,3},{1,0},{2,1},{3,2},{4,7},{5,4},{6,5},{7,6},{8,11},{9,8},{10,9... | collective-permute-start | bytes 1179656 | tf_op jit(solution)/shard_map/ppermute | solution.py:47
  34.0 5.3 %compare_select_fusion.refs_4_ = bf16[2048,2048]{1,0:T(8,128)(2,1)S(1)} fusion(bf16[2048,2048]{1,0:T(8,128)(2,1)} %param.5, s32[2048]{0:T(1024)S(1)} %copy-done.3), kind=kLoop, calls=%fused_computation | loop fusion | flops 8388608 | bytes 16785408 | tf_op jit(solution)/shard_map/jit(_where)/select_n | solution.py:72
  39.4 3.0 %collective-permute-done.1 = bf16[6,64,512]{2,1,0:T(8,128)(2,1)S(1)} collective-permute-done((bf16[6,64,512]{2,1,0:T(8,128)(2,1)S(1)}, bf16[6,64,512]{2,1,0:T(8,128)(2,1)S(1)}, u32[]{:S(2)}, u32[]{:S(2)}) %collective-permute-start.1) | collective-permute-done | bytes 393248 | tf_op jit(solution)/shard_map/ppermute | solution.py:47
  42.4 6.3 %collective-permute-done.2 = bf16[6,64,512]{2,1,0:T(8,128)(2,1)S(1)} collective-permute-done((bf16[6,64,512]{2,1,0:T(8,128)(2,1)S(1)}, bf16[6,64,512]{2,1,0:T(8,128)(2,1)S(1)}, u32[]{:S(2)}, u32[]{:S(2)}) %collective-permute-start.2) | collective-permute-done | bytes 393248 | tf_op jit(solution)/shard_map/ppermute | solution.py:47
  48.8 5.2 %ladder.1 = bf16[4,384,512]{2,1,0:T(8,128)(2,1)S(1)} custom-call(s32[4]{0:T(128)S(1)} %get-tuple-element.18.from_ref, s32[4]{0:T(128)S(1)} %get-tuple-element.17.to_ref, bf16[384,512]{1,0:T(8,128)(2,1)S(1)} %bitcast.23, bf16[384,512]{1,0:T(8,128)(2,1)S(1)} %bitcast.24, bf16[384,512]{1,0:T(8,128)(2,1)S(1)} %bitcast.25, bf16[384,512]{1,0:T(8,128)(2,1)S(1)} %bitcast.26, ...), custom_call_target="tpu_custom_call" | custom-call | flops 3221225472 | bytes 11534336 | tf_op jit(solution)/shard_map/ladder/pallas_call | solution.py:26
  53.9 1.2 fusion.5
  55.1 2.5 %collective-permute-start.3 = (bf16[6,64,512]{2,1,0:T(8,128)(2,1)}, bf16[6,64,512]{2,1,0:T(8,128)(2,1)}, u32[]{:S(2)}, u32[]{:S(2)}) collective-permute-start(bf16[6,64,512]{2,1,0:T(8,128)(2,1)} %bitcast.5), channel_id=1, source_target_pairs={{0,1},{1,2},{2,3},{3,0},{4,5},{5,6},{6,7},{7,4},{8,9},{9,10},{10,1... | collective-permute-start | bytes 1179656 | tf_op jit(solution)/shard_map/ppermute | solution.py:47
  57.7 3.0 %collective-permute-start.4 = (bf16[6,64,512]{2,1,0:T(8,128)(2,1)}, bf16[6,64,512]{2,1,0:T(8,128)(2,1)}, u32[]{:S(2)}, u32[]{:S(2)}) collective-permute-start(bf16[6,64,512]{2,1,0:T(8,128)(2,1)} %bitcast.6), channel_id=1, source_target_pairs={{0,2},{1,3},{2,0},{3,1},{4,6},{5,7},{6,4},{7,5},{8,10},{9,11},{10,... | collective-permute-start | bytes 1179656 | tf_op jit(solution)/shard_map/ppermute | solution.py:47
  60.7 3.9 %collective-permute-start.5 = (bf16[6,64,512]{2,1,0:T(8,128)(2,1)}, bf16[6,64,512]{2,1,0:T(8,128)(2,1)}, u32[]{:S(2)}, u32[]{:S(2)}) collective-permute-start(bf16[6,64,512]{2,1,0:T(8,128)(2,1)} %bitcast.7), channel_id=1, source_target_pairs={{0,3},{1,0},{2,1},{3,2},{4,7},{5,4},{6,5},{7,6},{8,11},{9,8},{10,9... | collective-permute-start | bytes 1179656 | tf_op jit(solution)/shard_map/ppermute | solution.py:47
  64.8 0.8 copy-done.2
  65.7 3.6 %collective-permute-done.3 = bf16[6,64,512]{2,1,0:T(8,128)(2,1)} collective-permute-done((bf16[6,64,512]{2,1,0:T(8,128)(2,1)}, bf16[6,64,512]{2,1,0:T(8,128)(2,1)}, u32[]{:S(2)}, u32[]{:S(2)}) %collective-permute-start.3) | collective-permute-done | bytes 393248 | tf_op jit(solution)/shard_map/ppermute | solution.py:47
  69.3 1.0 constant_dynamic-update-slice_fusion.2
  70.3 3.1 %collective-permute-done.4 = bf16[6,64,512]{2,1,0:T(8,128)(2,1)} collective-permute-done((bf16[6,64,512]{2,1,0:T(8,128)(2,1)}, bf16[6,64,512]{2,1,0:T(8,128)(2,1)}, u32[]{:S(2)}, u32[]{:S(2)}) %collective-permute-start.4) | collective-permute-done | bytes 393248 | tf_op jit(solution)/shard_map/ppermute | solution.py:47
  73.5 1.0 constant_dynamic-update-slice_fusion.1
  74.5 5.7 %collective-permute-done.5 = bf16[6,64,512]{2,1,0:T(8,128)(2,1)} collective-permute-done((bf16[6,64,512]{2,1,0:T(8,128)(2,1)}, bf16[6,64,512]{2,1,0:T(8,128)(2,1)}, u32[]{:S(2)}, u32[]{:S(2)}) %collective-permute-start.5) | collective-permute-done | bytes 393248 | tf_op jit(solution)/shard_map/ppermute | solution.py:47
  80.2 1.0 constant_dynamic-update-slice_fusion
  81.3 1.3 negate_convert_fusion
  82.5 0.9 copy.15
  83.4 75.0 %all_to_all.10 = bf16[32,6,8,512]{3,2,1,0:T(8,128)(2,1)S(1)} all-to-all(bf16[32,6,8,512]{3,2,1,0:T(8,128)(2,1)S(1)} %bitcast.27), channel_id=1, replica_groups=mesh['row'=32,'col'=6,'depth'=4] {'row'}, dimensions={0} | all-to-all | bytes 3145728 | tf_op jit(solution)/shard_map/all_to_all | solution.py:90
  158.4 1.6 fusion
  (13 shorter events, 0.3 us)
Async XLA Ops:
  0.0 81.3 %copy-start = (bf16[192,192]{1,0:T(8,128)(2,1)S(1)}, bf16[192,192]{1,0:T(8,128)(2,1)}, u32[]{:S(2)}) copy-start(bf16[192,192]{1,0:T(8,128)(2,1)} %param.7) | copy-start | bytes 221188
  2.8 20.6 %copy-start.1 = (bf16[6,256,512]{2,1,0:T(8,128)(2,1)S(1)}, bf16[6,256,512]{2,1,0:T(8,128)(2,1)}, u32[]{:S(2)}) copy-start(bf16[6,256,512]{2,1,0:T(8,128)(2,1)} %param.4) | copy-start | bytes 4718596
  2.8 78.5 %all-to-all-start = ((bf16[32,6,8,512]{3,2,1,0:T(8,128)(2,1)}), bf16[32,6,8,512]{3,2,1,0:T(8,128)(2,1)S(1)}, u32[]{:S(2)}, u32[]{:S(2)}) async-start(bf16[32,6,8,512]{3,2,1,0:T(8,128)(2,1)} %copy.13), calls=%async_computation | async-start | bytes 3145728 | tf_op jit(solution)/shard_map/all_to_all | solution.py:64
  23.4 10.6 %copy-start.3 = (s32[2048]{0:T(1024)S(1)}, s32[2048]{0:T(1024)}, u32[]{:S(2)}) copy-start(s32[2048]{0:T(1024)} %param.6) | copy-start | bytes 24580
  23.5 15.9 %collective-permute-start = (bf16[6,64,512]{2,1,0:T(8,128)(2,1)S(1)}, bf16[6,64,512]{2,1,0:T(8,128)(2,1)S(1)}, u32[]{:S(2)}, u32[]{:S(2)}) collective-permute-start(bf16[6,64,512]{2,1,0:T(8,128)(2,1)S(1)} %get-tuple-element.15), channel_id=1, source_target_pairs={{0,1},{1,2},{2,3},{3,0},{4,5},{5,6},{6,7},{7,4},{8,9},{9,10},{10,1... | collective-permute-start | bytes 1179656 | tf_op jit(solution)/shard_map/ppermute | solution.py:47
  26.9 15.5 %collective-permute-start.1 = (bf16[6,64,512]{2,1,0:T(8,128)(2,1)S(1)}, bf16[6,64,512]{2,1,0:T(8,128)(2,1)S(1)}, u32[]{:S(2)}, u32[]{:S(2)}) collective-permute-start(bf16[6,64,512]{2,1,0:T(8,128)(2,1)S(1)} %get-tuple-element.14), channel_id=1, source_target_pairs={{0,2},{1,3},{2,0},{3,1},{4,6},{5,7},{6,4},{7,5},{8,10},{9,11},{10,... | collective-permute-start | bytes 1179656 | tf_op jit(solution)/shard_map/ppermute | solution.py:47
  29.9 18.8 %collective-permute-start.2 = (bf16[6,64,512]{2,1,0:T(8,128)(2,1)S(1)}, bf16[6,64,512]{2,1,0:T(8,128)(2,1)S(1)}, u32[]{:S(2)}, u32[]{:S(2)}) collective-permute-start(bf16[6,64,512]{2,1,0:T(8,128)(2,1)S(1)} %get-tuple-element.13), channel_id=1, source_target_pairs={{0,3},{1,0},{2,1},{3,2},{4,7},{5,4},{6,5},{7,6},{8,11},{9,8},{10,9... | collective-permute-start | bytes 1179656 | tf_op jit(solution)/shard_map/ppermute | solution.py:47
  55.1 14.2 %collective-permute-start.3 = (bf16[6,64,512]{2,1,0:T(8,128)(2,1)}, bf16[6,64,512]{2,1,0:T(8,128)(2,1)}, u32[]{:S(2)}, u32[]{:S(2)}) collective-permute-start(bf16[6,64,512]{2,1,0:T(8,128)(2,1)} %bitcast.5), channel_id=1, source_target_pairs={{0,1},{1,2},{2,3},{3,0},{4,5},{5,6},{6,7},{7,4},{8,9},{9,10},{10,1... | collective-permute-start | bytes 1179656 | tf_op jit(solution)/shard_map/ppermute | solution.py:47
  57.7 15.8 %collective-permute-start.4 = (bf16[6,64,512]{2,1,0:T(8,128)(2,1)}, bf16[6,64,512]{2,1,0:T(8,128)(2,1)}, u32[]{:S(2)}, u32[]{:S(2)}) collective-permute-start(bf16[6,64,512]{2,1,0:T(8,128)(2,1)} %bitcast.6), channel_id=1, source_target_pairs={{0,2},{1,3},{2,0},{3,1},{4,6},{5,7},{6,4},{7,5},{8,10},{9,11},{10,... | collective-permute-start | bytes 1179656 | tf_op jit(solution)/shard_map/ppermute | solution.py:47
  60.7 19.6 %collective-permute-start.5 = (bf16[6,64,512]{2,1,0:T(8,128)(2,1)}, bf16[6,64,512]{2,1,0:T(8,128)(2,1)}, u32[]{:S(2)}, u32[]{:S(2)}) collective-permute-start(bf16[6,64,512]{2,1,0:T(8,128)(2,1)} %bitcast.7), channel_id=1, source_target_pairs={{0,3},{1,0},{2,1},{3,2},{4,7},{5,4},{6,5},{7,6},{8,11},{9,8},{10,9... | collective-permute-start | bytes 1179656 | tf_op jit(solution)/shard_map/ppermute | solution.py:47
  64.6 1.0 copy-start.2

commit v7 on v6

--- a/solution.py
+++ b/solution.py
@@ -1,3 +1,5 @@
+import functools
+
 import jax
 import jax.numpy as jnp
 from jax import lax
@@ -6,8 +8,8 @@
 from jax.sharding import PartitionSpec as P
 
 
-def ladder_kernel(from_ref, to_ref, *refs):
-    part_refs, masked_ref, out_ref = refs[:-2], refs[-2], refs[-1]
+def ladder_kernel(depth, from_ref, to_ref, *refs):
+    part_refs, masked_ref, out_refs = refs[:depth], refs[depth], refs[depth + 1 :]
     share = part_refs[0].shape[1]
     total = None
     for s, part_ref in enumerate(part_refs):
@@ -16,7 +18,11 @@
             part_ref[...], masked_ref[pl.ds(start, share), :], preferred_element_type=jnp.float32
         )
         total = term if total is None else total + term
-    out_ref[0] = total.astype(out_ref.dtype)
+    for t, out_ref in enumerate(out_refs):
+
+        @pl.when(pl.program_id(0) == t)
+        def _():
+            out_ref[...] = total.astype(out_ref.dtype)
 
 
 def ladder_product(came_from, goes_to, parts, masked):
@@ -24,15 +30,15 @@
     rows, share = parts[0].shape
     whole_pairs = masked.shape[0]
     return pl.pallas_call(
-        ladder_kernel,
+        functools.partial(ladder_kernel, depth),
         grid_spec=pltpu.PrefetchScalarGridSpec(
             num_scalar_prefetch=2,
             grid=(depth,),
             in_specs=[pl.BlockSpec((rows, share), lambda t, came, goes: (0, 0))] * depth
             + [pl.BlockSpec((whole_pairs, share), lambda t, came, goes: (0, goes[t]))],
-            out_specs=pl.BlockSpec((1, rows, share), lambda t, came, goes: (t, 0, 0)),
+            out_specs=[pl.BlockSpec((rows, share), lambda t, came, goes: (0, 0))] * depth,
         ),
-        out_shape=jax.ShapeDtypeStruct((depth, rows, share), jnp.bfloat16),
+        out_shape=[jax.ShapeDtypeStruct((rows, share), jnp.bfloat16)] * depth,
         compiler_params=pltpu.CompilerParams(vmem_limit_bytes=24 * 1024 * 1024),
         cost_estimate=pl.CostEstimate(
             flops=2 * rows * whole_pairs * whole_pairs,
@@ -72,14 +78,15 @@
     masked = jnp.where(same, integrals, jnp.zeros_like(integrals))
     columns = ladder_product(
         came_from, goes_to, [part.reshape(local_i * part_j, share) for part in parts], masked
-    ).reshape(depth, local_i, part_j, share)
+    )
     ladder = jnp.zeros_like(amplitudes)
     for t in range(depth):
-        piece = columns[0] if t == 0 else shift(columns[t], depth, t)
+        piece = columns[t].reshape(local_i, part_j, share)
+        piece = piece if t == 0 else shift(piece, depth, t)
         start = ((here - t + depth) % depth) * part_j
         ladder = lax.dynamic_update_slice(ladder, piece, (0, start, 0))
 
-    tied_fock, ladder = lax.optimization_barrier((occ_fock, ladder))
+    tied_fock, _ = lax.optimization_barrier((occ_fock, columns[0]))
     product = jnp.einsum(
         "ik,kmn->imn",
         tied_fock,

time: 161 us -> 169 us (1.050)
  the two profiles are of different devices: /device:TPU:10 before, /device:TPU:141 now
where the time goes in v7:
time: 169 us; the launch traced here: 168 us
  waiting for transfers between devices  101 us (60%)
  starting transfers between devices  40.2 us (24%)
  local copies, waits for them, and re-layouts  12.3 us (7%)
  other arithmetic  8.33 us (5%)
  Pallas kernels  5.36 us (3%)
    all_to_all x1, waiting for transfers between devices, on_device(): dressed = lax.all_to_all(dressed_part, 'row', split_axis=0, concat_axis=0)  45.9 us
    all_to_all x1, waiting for transfers between devices, on_device(): arrived = lax.all_to_all(blocks, 'row', split_axis=0, concat_axis=0)  33.8 us
    ppermute x6, waiting for transfers between devices, shift(): lax.ppermute(block, 'depth', [(d, (d + step) % depth) for d in range(dept...  21 us
    all_to_all x1, starting transfers between devices, on_device(): arrived = lax.all_to_all(blocks, 'row', split_axis=0, concat_axis=0)  17.6 us
    ppermute x6, starting transfers between devices, shift(): lax.ppermute(block, 'depth', [(d, (d + step) % depth) for d in range(dept...  16 us
    all_to_all x1, starting transfers between devices, on_device(): dressed = lax.all_to_all(dressed_part, 'row', split_axis=0, concat_axis=0)  6.63 us
    dynamic_update_slice x4, local copies, waits for them, and re-layouts, on_device(): ladder = lax.dynamic_update_slice(ladder, piece, (0, start, 0))  6.09 us
    pallas_call x1, Pallas kernels, ladder_product(): pl.pallas_call(functools.partial(ladder_kernel, depth), grid_spec=pltpu.P...  5.36 us
  transfers between devices with their start and end apart: 8, of which 7 were waited for; matrix products, arithmetic and copies ran while one was open for 8% of the time, Pallas kernels for 3%

profile of v7, /device:TPU:141, one launch (start us, length us, event | category | flops | bytes accessed | tf_op | source)
XLA Modules:
  0.0 168.5 jit_solution(6751479226608775264)
XLA Ops:
  0.0 2.8 %copy.13 = bf16[32,6,8,512]{3,2,1,0:T(8,128)(2,1)} copy(bf16[32,6,8,512]{3,2,0,1:T(8,128)(2,1)} %bitcast.31) | data formatting | bytes 3145728 | tf_op jit(solution)/shard_map/transpose | solution.py:69
  2.8 17.6 %all-to-all-start = ((bf16[32,6,8,512]{3,2,1,0:T(8,128)(2,1)}), bf16[32,6,8,512]{3,2,1,0:T(8,128)(2,1)S(1)}, u32[]{:S(2)}, u32[]{:S(2)}) async-start(bf16[32,6,8,512]{3,2,1,0:T(8,128)(2,1)} %copy.13), calls=%async_computation | async-start | bytes 3145728 | tf_op jit(solution)/shard_map/all_to_all | solution.py:70
  20.6 2.8 %collective-permute-start = (bf16[6,64,512]{2,1,0:T(8,128)(2,1)S(1)}, bf16[6,64,512]{2,1,0:T(8,128)(2,1)S(1)}, u32[]{:S(2)}, u32[]{:S(2)}) collective-permute-start(bf16[6,64,512]{2,1,0:T(8,128)(2,1)S(1)} %get-tuple-element.17), channel_id=1, source_target_pairs={{0,1},{1,2},{2,3},{3,0},{4,5},{5,6},{6,7},{7,4},{8,9},{9,10},{10,1... | collective-permute-start | bytes 1179656 | tf_op jit(solution)/shard_map/ppermute | solution.py:53
  23.4 2.4 %collective-permute-start.1 = (bf16[6,64,512]{2,1,0:T(8,128)(2,1)S(1)}, bf16[6,64,512]{2,1,0:T(8,128)(2,1)S(1)}, u32[]{:S(2)}, u32[]{:S(2)}) collective-permute-start(bf16[6,64,512]{2,1,0:T(8,128)(2,1)S(1)} %get-tuple-element.16), channel_id=1, source_target_pairs={{0,2},{1,3},{2,0},{3,1},{4,6},{5,7},{6,4},{7,5},{8,10},{9,11},{10,... | collective-permute-start | bytes 1179656 | tf_op jit(solution)/shard_map/ppermute | solution.py:53
  25.8 2.8 %collective-permute-start.2 = (bf16[6,64,512]{2,1,0:T(8,128)(2,1)S(1)}, bf16[6,64,512]{2,1,0:T(8,128)(2,1)S(1)}, u32[]{:S(2)}, u32[]{:S(2)}) collective-permute-start(bf16[6,64,512]{2,1,0:T(8,128)(2,1)S(1)} %get-tuple-element.15), channel_id=1, source_target_pairs={{0,3},{1,0},{2,1},{3,2},{4,7},{5,4},{6,5},{7,6},{8,11},{9,8},{10,9... | collective-permute-start | bytes 1179656 | tf_op jit(solution)/shard_map/ppermute | solution.py:53
  28.6 5.3 %compare_select_fusion.refs_4_ = bf16[2048,2048]{1,0:T(8,128)(2,1)S(1)} fusion(bf16[2048,2048]{1,0:T(8,128)(2,1)} %param.5, s32[2048]{0:T(1024)S(1)} %copy-done.2), kind=kLoop, calls=%fused_computation | loop fusion | flops 8388608 | bytes 16785408 | tf_op jit(solution)/shard_map/jit(_where)/select_n | solution.py:78
  34.0 6.2 %collective-permute-done.1 = bf16[6,64,512]{2,1,0:T(8,128)(2,1)S(1)} collective-permute-done((bf16[6,64,512]{2,1,0:T(8,128)(2,1)S(1)}, bf16[6,64,512]{2,1,0:T(8,128)(2,1)S(1)}, u32[]{:S(2)}, u32[]{:S(2)}) %collective-permute-start.1) | collective-permute-done | bytes 393248 | tf_op jit(solution)/shard_map/ppermute | solution.py:53
  40.2 4.4 %collective-permute-done.2 = bf16[6,64,512]{2,1,0:T(8,128)(2,1)S(1)} collective-permute-done((bf16[6,64,512]{2,1,0:T(8,128)(2,1)S(1)}, bf16[6,64,512]{2,1,0:T(8,128)(2,1)S(1)}, u32[]{:S(2)}, u32[]{:S(2)}) %collective-permute-start.2) | collective-permute-done | bytes 393248 | tf_op jit(solution)/shard_map/ppermute | solution.py:53
  44.6 5.4 %ladder.1 = (bf16[384,512]{1,0:T(8,128)(2,1)S(1)}, bf16[384,512]{1,0:T(8,128)(2,1)S(1)}, bf16[384,512]{1,0:T(8,128)(2,1)S(1)}, bf16[384,512]{1,0:T(8,128)(2,1)S(1)}) custom-call(s32[4]{0:T(128)S(1)} %get-tuple-element.20.from_ref, s32[4]{0:T(128)S(1)} %get-tuple-element.19.to_ref, bf16[384,512]{1,0:T(8,128)(2,1)S(1)} %bitcast.24, ...), custom_call_target="tpu_custom_call" | custom-call | flops 3221225472 | bytes 11534336 | tf_op jit(solution)/shard_map/ladder/pallas_call | solution.py:32
  50.0 33.8 %all-to-all-done = bf16[32,6,8,512]{3,2,1,0:T(8,128)(2,1)S(1)} async-done(((bf16[32,6,8,512]{3,2,1,0:T(8,128)(2,1)}), bf16[32,6,8,512]{3,2,1,0:T(8,128)(2,1)S(1)}, u32[]{:S(2)}, u32[]{:S(2)}) %all-to-all-start) | async-done | bytes 1572896 | tf_op jit(solution)/shard_map/all_to_all | solution.py:70
  83.8 1.3 negate_convert_fusion
  85.1 2.0 %copy.15 = bf16[192,8,512]{2,1,0:T(8,128)(2,1)} copy(bf16[192,8,512]{2,0,1:T(8,128)(2,1)S(1)} %negate_convert_fusion) | data formatting | bytes 3145728 | tf_op jit(solution)/shard_map/convert_element_type | solution.py:96
  87.1 6.6 %all-to-all-start.1 = ((bf16[32,6,8,512]{3,2,1,0:T(8,128)(2,1)}), bf16[32,6,8,512]{3,2,1,0:T(8,128)(2,1)S(1)}, u32[]{:S(2)}, u32[]{:S(2)}) async-start(bf16[32,6,8,512]{3,2,1,0:T(8,128)(2,1)} %bitcast.12), calls=%async_computation.1 | async-start | bytes 3145728 | tf_op jit(solution)/shard_map/all_to_all | solution.py:97
  93.8 2.8 %collective-permute-start.3 = (bf16[6,64,512]{2,1,0:T(8,128)(2,1)S(1)}, bf16[6,64,512]{2,1,0:T(8,128)(2,1)}, u32[]{:S(2)}, u32[]{:S(2)}) collective-permute-start(bf16[6,64,512]{2,1,0:T(8,128)(2,1)S(1)} %bitcast.27), channel_id=1, source_target_pairs={{0,1},{1,2},{2,3},{3,0},{4,5},{5,6},{6,7},{7,4},{8,9},{9,10},{10,1... | collective-permute-start | bytes 1179656 | tf_op jit(solution)/shard_map/ppermute | solution.py:53
  96.6 2.4 %collective-permute-start.4 = (bf16[6,64,512]{2,1,0:T(8,128)(2,1)S(1)}, bf16[6,64,512]{2,1,0:T(8,128)(2,1)}, u32[]{:S(2)}, u32[]{:S(2)}) collective-permute-start(bf16[6,64,512]{2,1,0:T(8,128)(2,1)S(1)} %bitcast.26), channel_id=1, source_target_pairs={{0,2},{1,3},{2,0},{3,1},{4,6},{5,7},{6,4},{7,5},{8,10},{9,11},{10,... | collective-permute-start | bytes 1179656 | tf_op jit(solution)/shard_map/ppermute | solution.py:53
  99.0 2.8 %collective-permute-start.5 = (bf16[6,64,512]{2,1,0:T(8,128)(2,1)S(1)}, bf16[6,64,512]{2,1,0:T(8,128)(2,1)}, u32[]{:S(2)}, u32[]{:S(2)}) collective-permute-start(bf16[6,64,512]{2,1,0:T(8,128)(2,1)S(1)} %bitcast.25), channel_id=1, source_target_pairs={{0,3},{1,0},{2,1},{3,2},{4,7},{5,4},{6,5},{7,6},{8,11},{9,8},{10,9... | collective-permute-start | bytes 1179656 | tf_op jit(solution)/shard_map/ppermute | solution.py:53
  101.8 1.3 broadcast_in_dim.8
  104.4 1.8 %constant_dynamic-update-slice_fusion.2 = bf16[6,256,512]{2,1,0:T(8,128)(2,1)} fusion(bf16[6,256,512]{2,1,0:T(8,128)(2,1)} %constant_dynamic-update-slice_fusion.3, bf16[6,64,512]{2,1,0:T(8,128)(2,1)} %collective-permute-done.3, s32[]{:T(128)S(6)} %select_n.70), kind=kLoop, calls=%fused_computation.13 | loop fusion | bytes 786436 | tf_op jit(solution)/shard_map/dynamic_update_slice | solution.py:87
  106.1 6.6 %collective-permute-done.4 = bf16[6,64,512]{2,1,0:T(8,128)(2,1)} collective-permute-done((bf16[6,64,512]{2,1,0:T(8,128)(2,1)S(1)}, bf16[6,64,512]{2,1,0:T(8,128)(2,1)}, u32[]{:S(2)}, u32[]{:S(2)}) %collective-permute-start.4) | collective-permute-done | bytes 393248 | tf_op jit(solution)/shard_map/ppermute | solution.py:53
  112.7 1.8 %constant_dynamic-update-slice_fusion.1 = bf16[6,256,512]{2,1,0:T(8,128)(2,1)} fusion(bf16[6,256,512]{2,1,0:T(8,128)(2,1)} %constant_dynamic-update-slice_fusion.2, bf16[6,64,512]{2,1,0:T(8,128)(2,1)} %collective-permute-done.4, s32[]{:T(128)S(6)} %select_n.68), kind=kLoop, calls=%fused_computation.12 | loop fusion | bytes 786436 | tf_op jit(solution)/shard_map/dynamic_update_slice | solution.py:87
  114.5 3.3 %collective-permute-done.5 = bf16[6,64,512]{2,1,0:T(8,128)(2,1)} collective-permute-done((bf16[6,64,512]{2,1,0:T(8,128)(2,1)S(1)}, bf16[6,64,512]{2,1,0:T(8,128)(2,1)}, u32[]{:S(2)}, u32[]{:S(2)}) %collective-permute-start.5) | collective-permute-done | bytes 393248 | tf_op jit(solution)/shard_map/ppermute | solution.py:53
  117.8 1.8 %constant_dynamic-update-slice_fusion = bf16[6,256,512]{2,1,0:T(8,128)(2,1)} fusion(bf16[6,256,512]{2,1,0:T(8,128)(2,1)} %constant_dynamic-update-slice_fusion.1, bf16[6,64,512]{2,1,0:T(8,128)(2,1)} %collective-permute-done.5, s32[]{:T(128)S(6)} %select_n.66), kind=kLoop, calls=%fused_computation.11 | loop fusion | bytes 786436 | tf_op jit(solution)/shard_map/dynamic_update_slice | solution.py:87
  119.6 45.9 %all-to-all-done.1 = bf16[32,6,8,512]{3,2,1,0:T(8,128)(2,1)S(1)} async-done(((bf16[32,6,8,512]{3,2,1,0:T(8,128)(2,1)}), bf16[32,6,8,512]{3,2,1,0:T(8,128)(2,1)S(1)}, u32[]{:S(2)}, u32[]{:S(2)}) %all-to-all-start.1) | async-done | bytes 1572896 | tf_op jit(solution)/shard_map/all_to_all | solution.py:97
  165.5 3.0 %fusion = bf16[6,256,512]{2,1,0:T(8,128)(2,1)} fusion(bf16[6,256,512]{2,1,0:T(8,128)(2,1)} %constant_dynamic-update-slice_fusion, bf16[32,6,8,512]{3,2,1,0:T(8,128)(2,1)S(1)} %all-to-all-done.1), kind=kLoop, calls=%fused_computation.2 | loop fusion | flops 3145728 | bytes 4718592 | tf_op jit(solution)/shard_map/convert_element_type | solution.py:99
  (11 shorter events, 1.4 us)
Async XLA Ops:
  0.0 83.8 %copy-start = (bf16[192,192]{1,0:T(8,128)(2,1)S(1)}, bf16[192,192]{1,0:T(8,128)(2,1)}, u32[]{:S(2)}) copy-start(bf16[192,192]{1,0:T(8,128)(2,1)} %param.7) | copy-start | bytes 221188
  2.8 17.6 %copy-start.1 = (bf16[6,256,512]{2,1,0:T(8,128)(2,1)S(1)}, bf16[6,256,512]{2,1,0:T(8,128)(2,1)}, u32[]{:S(2)}) copy-start(bf16[6,256,512]{2,1,0:T(8,128)(2,1)} %param.4) | copy-start | bytes 4718596
  2.8 81.0 %all-to-all-start = ((bf16[32,6,8,512]{3,2,1,0:T(8,128)(2,1)}), bf16[32,6,8,512]{3,2,1,0:T(8,128)(2,1)S(1)}, u32[]{:S(2)}, u32[]{:S(2)}) async-start(bf16[32,6,8,512]{3,2,1,0:T(8,128)(2,1)} %copy.13), calls=%async_computation | async-start | bytes 3145728 | tf_op jit(solution)/shard_map/all_to_all | solution.py:70
  20.4 8.2 %copy-start.2 = (s32[2048]{0:T(1024)S(1)}, s32[2048]{0:T(1024)}, u32[]{:S(2)}) copy-start(s32[2048]{0:T(1024)} %param.6) | copy-start | bytes 24580
  20.6 13.4 %collective-permute-start = (bf16[6,64,512]{2,1,0:T(8,128)(2,1)S(1)}, bf16[6,64,512]{2,1,0:T(8,128)(2,1)S(1)}, u32[]{:S(2)}, u32[]{:S(2)}) collective-permute-start(bf16[6,64,512]{2,1,0:T(8,128)(2,1)S(1)} %get-tuple-element.17), channel_id=1, source_target_pairs={{0,1},{1,2},{2,3},{3,0},{4,5},{5,6},{6,7},{7,4},{8,9},{9,10},{10,1... | collective-permute-start | bytes 1179656 | tf_op jit(solution)/shard_map/ppermute | solution.py:53
  23.4 16.8 %collective-permute-start.1 = (bf16[6,64,512]{2,1,0:T(8,128)(2,1)S(1)}, bf16[6,64,512]{2,1,0:T(8,128)(2,1)S(1)}, u32[]{:S(2)}, u32[]{:S(2)}) collective-permute-start(bf16[6,64,512]{2,1,0:T(8,128)(2,1)S(1)} %get-tuple-element.16), channel_id=1, source_target_pairs={{0,2},{1,3},{2,0},{3,1},{4,6},{5,7},{6,4},{7,5},{8,10},{9,11},{10,... | collective-permute-start | bytes 1179656 | tf_op jit(solution)/shard_map/ppermute | solution.py:53
  25.8 18.8 %collective-permute-start.2 = (bf16[6,64,512]{2,1,0:T(8,128)(2,1)S(1)}, bf16[6,64,512]{2,1,0:T(8,128)(2,1)S(1)}, u32[]{:S(2)}, u32[]{:S(2)}) collective-permute-start(bf16[6,64,512]{2,1,0:T(8,128)(2,1)S(1)} %get-tuple-element.15), channel_id=1, source_target_pairs={{0,3},{1,0},{2,1},{3,2},{4,7},{5,4},{6,5},{7,6},{8,11},{9,8},{10,9... | collective-permute-start | bytes 1179656 | tf_op jit(solution)/shard_map/ppermute | solution.py:53
  87.1 78.4 %all-to-all-start.1 = ((bf16[32,6,8,512]{3,2,1,0:T(8,128)(2,1)}), bf16[32,6,8,512]{3,2,1,0:T(8,128)(2,1)S(1)}, u32[]{:S(2)}, u32[]{:S(2)}) async-start(bf16[32,6,8,512]{3,2,1,0:T(8,128)(2,1)} %bitcast.12), calls=%async_computation.1 | async-start | bytes 3145728 | tf_op jit(solution)/shard_map/all_to_all | solution.py:97
  93.8 10.6 %collective-permute-start.3 = (bf16[6,64,512]{2,1,0:T(8,128)(2,1)S(1)}, bf16[6,64,512]{2,1,0:T(8,128)(2,1)}, u32[]{:S(2)}, u32[]{:S(2)}) collective-permute-start(bf16[6,64,512]{2,1,0:T(8,128)(2,1)S(1)} %bitcast.27), channel_id=1, source_target_pairs={{0,1},{1,2},{2,3},{3,0},{4,5},{5,6},{6,7},{7,4},{8,9},{9,10},{10,1... | collective-permute-start | bytes 1179656 | tf_op jit(solution)/shard_map/ppermute | solution.py:53
  96.6 16.2 %collective-permute-start.4 = (bf16[6,64,512]{2,1,0:T(8,128)(2,1)S(1)}, bf16[6,64,512]{2,1,0:T(8,128)(2,1)}, u32[]{:S(2)}, u32[]{:S(2)}) collective-permute-start(bf16[6,64,512]{2,1,0:T(8,128)(2,1)S(1)} %bitcast.26), channel_id=1, source_target_pairs={{0,2},{1,3},{2,0},{3,1},{4,6},{5,7},{6,4},{7,5},{8,10},{9,11},{10,... | collective-permute-start | bytes 1179656 | tf_op jit(solution)/shard_map/ppermute | solution.py:53
  99.0 18.8 %collective-permute-start.5 = (bf16[6,64,512]{2,1,0:T(8,128)(2,1)S(1)}, bf16[6,64,512]{2,1,0:T(8,128)(2,1)}, u32[]{:S(2)}, u32[]{:S(2)}) collective-permute-start(bf16[6,64,512]{2,1,0:T(8,128)(2,1)S(1)} %bitcast.25), channel_id=1, source_target_pairs={{0,3},{1,0},{2,1},{3,2},{4,7},{5,4},{6,5},{7,6},{8,11},{9,8},{10,9... | collective-permute-start | bytes 1179656 | tf_op jit(solution)/shard_map/ppermute | solution.py:53
